TPU v7x, 512 devices: a whole 4x4x16 slice. The times are simulated.
512 devices in a mesh: dp: 8 (over x, core), expert: 64 (over y, z).
Axes of the slice: x: 4, y: 4, z: 16, core: 2. Of those that a mesh axis runs over, the one named last changes fastest.
Arguments:
- tokens: bfloat16 [8192, 3584], P(('dp', 'expert')), may hold values from -6 to 6
- cotangent: bfloat16 [8192, 3584], P(('dp', 'expert')), may hold values from -6 to 6
- expert_ids: int32 [8192, 2], P(('dp', 'expert')), may hold values from 0 to 7, all different within a row; in each aligned block of 16 rows (0 to 15, 16 to 31, ...) at most 8 rows name the same one
- gates: bfloat16 [8192, 2], P(('dp', 'expert')), may hold values from 0.049804688 to 1
- w_gate: bfloat16 [64, 3584, 128], P('expert', 'dp'), may hold values from -0.09375 to 0.09375
- w_up: bfloat16 [64, 3584, 128], P('expert', 'dp'), may hold values from -0.09375 to 0.09375
- w_down_t: bfloat16 [64, 3584, 128], P('expert', 'dp'), may hold values from -0.1875 to 0.1875
Outputs:
- grad_tokens: bfloat16 [8192, 3584], P(('dp', 'expert'))
- grad_gates: float32 [8192, 2], P(('dp', 'expert'))
- grad_w_gate: bfloat16 [64, 3584, 128], P('expert', 'dp')
- grad_w_up: bfloat16 [64, 3584, 128], P('expert', 'dp')
- grad_w_down_t: bfloat16 [64, 3584, 128], P('expert', 'dp')
Inputs may be any that keep to these rules, and one draw needn't show every extreme that they name: `expert_ids`: each row names 2 different experts; among the 16 rows of one device no expert is named more than 8 times, a bound that some block reaches.
All inputs are finite; a program needn't handle non-finite values.
Results may differ from a plain program's by a relative error of at most 0.02.
Values may be sent and summed in bfloat16 or wider, within the bound.
A program may use at most 64 MiB of HBM per device.

v0:
```python
import jax
import jax.numpy as jnp
from jax import lax
from jax.sharding import PartitionSpec as P

GROUP = 8


def mult(left, right):
    return jnp.dot(left, right, preferred_element_type=jnp.float32)


def mult_back(left, right):
    return lax.dot_general(
        left, right, (((1,), (1,)), ((), ())), preferred_element_type=jnp.float32
    )


def mult_down(left, right):
    return lax.dot_general(
        left, right, (((0,), (0,)), ((), ())), preferred_element_type=jnp.float32
    )


def shards(tokens, cotangent, expert_ids, gates, w_gate, w_up, w_down_t):
    nexp = lax.axis_size("expert")
    group = GROUP
    expert_count = nexp // group
    tok_rows, width = tokens.shape
    top = expert_ids.shape[1]
    cap = tok_rows // 2
    total_slots = nexp * cap
    flat_ids = expert_ids.reshape(-1)
    onehot = (flat_ids[:, None] == jnp.arange(expert_count, dtype=jnp.int32)[None, :]).astype(
        jnp.int32
    )
    before = jnp.cumsum(onehot, axis=0) - onehot
    slot = jnp.sum(before * onehot, axis=1)
    target = flat_ids * cap + slot
    place = target[None, :] == jnp.arange(expert_count * cap, dtype=jnp.int32)[:, None]
    place_tok = jnp.any(place.reshape(expert_count * cap, tok_rows, top), axis=2).astype(
        jnp.bfloat16
    )
    slot_x = mult(place_tok, tokens).astype(jnp.bfloat16)
    slot_dy = mult(place_tok, cotangent).astype(jnp.bfloat16)
    slot_p = mult(place.astype(jnp.bfloat16), gates.reshape(-1, 1))[:, 0].astype(jnp.bfloat16)
    send_x = jnp.repeat(slot_x.reshape(expert_count, cap, width), group, axis=0)
    send_dy = jnp.repeat(slot_dy.reshape(expert_count, cap, width), group, axis=0)
    send_p = jnp.repeat(slot_p.reshape(expert_count, cap), group, axis=0)
    got_x, got_dy, got_p = (
        lax.all_to_all(send_x, "expert", split_axis=0, concat_axis=0, tiled=True),
        lax.all_to_all(send_dy, "expert", split_axis=0, concat_axis=0, tiled=True),
        lax.all_to_all(send_p, "expert", split_axis=0, concat_axis=0, tiled=True),
    )
    rows_x = got_x.reshape(total_slots, width)
    rows_dy = got_dy.reshape(total_slots, width)
    rows_p = got_p.reshape(total_slots)
    gate_rows = w_gate[0]
    up_rows = w_up[0]
    down_rows = w_down_t[0]
    ffh = gate_rows.shape[1]
    full_gate, full_up, full_down = (
        lax.all_gather(gate_rows, "dp", axis=0, tiled=True),
        lax.all_gather(up_rows, "dp", axis=0, tiled=True),
        lax.all_gather(down_rows, "dp", axis=0, tiled=True),
    )
    pre_gate = mult(rows_x, full_gate)
    pre_up = mult(rows_x, full_up)
    back = mult(rows_dy, full_down)
    sig = jax.nn.sigmoid(pre_gate)
    silu = pre_gate * sig
    hidden = (silu * pre_up).astype(jnp.bfloat16)
    weight = rows_p.astype(jnp.float32)[:, None]
    d_hidden = weight * back
    part_gate = jnp.sum(hidden.astype(jnp.float32) * back, axis=1).astype(jnp.bfloat16)
    d_gate = (d_hidden * pre_up * sig * (1.0 + pre_gate * (1.0 - sig))).astype(jnp.bfloat16)
    d_up = (d_hidden * silu).astype(jnp.bfloat16)
    scaled = (weight * rows_dy.astype(jnp.float32)).astype(jnp.bfloat16)
    part_tokens = (mult_back(d_gate, full_gate) + mult_back(d_up, full_up)).astype(jnp.bfloat16)
    joined = jnp.concatenate([d_gate, d_up], axis=1)
    summed = lax.psum_scatter(
        jnp.concatenate([mult_down(rows_x, joined), mult_down(scaled, hidden)], axis=1).astype(
            jnp.bfloat16
        ),
        "dp",
        scatter_dimension=0,
        tiled=True,
    ).astype(jnp.float32)
    grad_w_gate = summed[:, :ffh].astype(jnp.bfloat16)[None]
    grad_w_up = summed[:, ffh : 2 * ffh].astype(jnp.bfloat16)[None]
    grad_w_down_t = summed[:, 2 * ffh :].astype(jnp.bfloat16)[None]
    back_x = part_tokens.reshape(nexp, cap, width)
    back_p = part_gate.reshape(nexp, cap)
    ret_x, ret_p = (
        lax.all_to_all(back_x, "expert", split_axis=0, concat_axis=0, tiled=True),
        lax.all_to_all(back_p, "expert", split_axis=0, concat_axis=0, tiled=True),
    )
    ret_x = ret_x.reshape(total_slots, width)
    ret_p = ret_p.reshape(total_slots)
    own_expert = expert_ids[:, :, None]
    own_slot = slot.reshape(tok_rows, top)[:, :, None]
    member = jnp.arange(group, dtype=jnp.int32)[None, None, :]
    source = (own_expert * group + member) * cap + own_slot
    match = source[..., None] == jnp.arange(total_slots, dtype=jnp.int32)[None, None, None, :]
    combine = jnp.sum(match.astype(jnp.bfloat16), axis=(1, 2))
    grad_tokens = mult(combine, ret_x).astype(jnp.bfloat16)
    grad_gates = jnp.sum(
        match.astype(jnp.float32) * ret_p.astype(jnp.float32)[None, None, None, :], axis=(2, 3)
    )
    return (grad_tokens, grad_gates, grad_w_gate, grad_w_up, grad_w_down_t)


def solution(mesh):
    return jax.shard_map(
        shards,
        mesh=mesh,
        in_specs=(
            P(("dp", "expert"), None),
            P(("dp", "expert"), None),
            P(("dp", "expert"), None),
            P(("dp", "expert"), None),
            P("expert", "dp", None),
            P("expert", "dp", None),
            P("expert", "dp", None),
        ),
        out_specs=(
            P(("dp", "expert"), None),
            P(("dp", "expert"), None),
            P("expert", "dp", None),
            P("expert", "dp", None),
            P("expert", "dp", None),
        ),
        check_vma=False,
    )
```

profile of v0, /device:TPU:1, one launch (start us, length us, event | category | flops | bytes accessed | tf_op | source)
XLA Modules:
  0.0 598.1 jit_solution(2024819233011589236)
XLA Ops:
  7.2 0.8 copy.39
  8.4 0.7 copy.41
  9.8 0.7 copy.42
  10.5 19.3 %all-to-all-start = ((bf16[64,1,8]{2,1,0:T(2,128)(2,1)}), bf16[64,1,8]{2,1,0:T(2,128)(2,1)S(1)}, u32[]{:S(2)}, u32[]{:S(2)}) async-start(bf16[64,1,8]{2,1,0:T(2,128)(2,1)} %copy.42), calls=%async_computation | async-start | bytes 65536 | tf_op jit(solution)/shard_map/all_to_all | solution.py:53
  30.4 12.6 %all-to-all-done = bf16[64,1,8]{2,1,0:T(2,128)(2,1)S(1)} async-done(((bf16[64,1,8]{2,1,0:T(2,128)(2,1)}), bf16[64,1,8]{2,1,0:T(2,128)(2,1)S(1)}, u32[]{:S(2)}, u32[]{:S(2)}) %all-to-all-start) | async-done | bytes 1056 | tf_op jit(solution)/shard_map/all_to_all | solution.py:53
  43.0 2.1 broadcast_in_dim.14
  45.1 5.7 all-to-all-start.2
  51.1 159.0 %all-to-all-done.2 = bf16[64,8,3584]{2,1,0:T(8,128)(2,1)} async-done(((bf16[64,8,3584]{2,1,0:T(8,128)(2,1)}), bf16[64,8,3584]{2,1,0:T(8,128)(2,1)}, u32[]{:S(2)}, u32[]{:S(2)}) %all-to-all-start.2) | async-done | bytes 3670048 | tf_op jit(solution)/shard_map/all_to_all | solution.py:51
  210.2 2.1 broadcast_in_dim.13
  212.2 13.8 %all-to-all-start.1 = ((bf16[64,8,3584]{2,1,0:T(8,128)(2,1)}), bf16[64,8,3584]{2,1,0:T(8,128)(2,1)}, u32[]{:S(2)}, u32[]{:S(2)}) async-start(bf16[64,8,3584]{2,1,0:T(8,128)(2,1)} %bitcast.60), calls=%async_computation.1 | async-start | bytes 7340032 | tf_op jit(solution)/shard_map/all_to_all | solution.py:52
  226.0 14.8 %all-gather.2 = bf16[1,3584,128]{2,1,0:T(8,128)(2,1)S(1)} all-gather(bf16[1,448,128]{2,1,0:T(8,128)(2,1)S(1)} %copy-done.3), channel_id=4, replica_groups=mesh['dp'=8,'expert'=64] {'dp'}, dimensions={1}, use_global_device_ids=true | all-gather | bytes 1032192 | tf_op jit(solution)/shard_map/all_gather | solution.py:63
  240.8 13.5 %all-gather.1 = bf16[1,3584,128]{2,1,0:T(8,128)(2,1)S(1)} all-gather(bf16[1,448,128]{2,1,0:T(8,128)(2,1)S(1)} %copy-done.4), channel_id=3, replica_groups=mesh['dp'=8,'expert'=64] {'dp'}, dimensions={1}, use_global_device_ids=true | all-gather | bytes 1032192 | tf_op jit(solution)/shard_map/all_gather | solution.py:64
  254.3 13.5 %all-gather = bf16[1,3584,128]{2,1,0:T(8,128)(2,1)S(1)} all-gather(bf16[1,448,128]{2,1,0:T(8,128)(2,1)S(1)} %copy-done.5), channel_id=2, replica_groups=mesh['dp'=8,'expert'=64] {'dp'}, dimensions={1}, use_global_device_ids=true | all-gather | bytes 1032192 | tf_op jit(solution)/shard_map/all_gather | solution.py:65
  268.0 3.4 fusion.5
  271.4 3.4 fusion.7
  274.8 110.2 %all-to-all-done.1 = bf16[64,8,3584]{2,1,0:T(8,128)(2,1)} async-done(((bf16[64,8,3584]{2,1,0:T(8,128)(2,1)}), bf16[64,8,3584]{2,1,0:T(8,128)(2,1)}, u32[]{:S(2)}, u32[]{:S(2)}) %all-to-all-start.1) | async-done | bytes 3670048 | tf_op jit(solution)/shard_map/all_to_all | solution.py:52
  385.0 4.1 multiply_reduce_fusion
  389.1 4.1 fusion.13
  394.0 13.5 %all-to-all-start.4 = ((bf16[64,1,8]{2,1,0:T(2,128)(2,1)}), bf16[64,1,8]{2,1,0:T(2,128)(2,1)S(1)}, u32[]{:S(2)}, u32[]{:S(2)}) async-start(bf16[64,1,8]{2,1,0:T(2,128)(2,1)} %convert_element_type.105), calls=%async_computation.4 | async-start | bytes 65536 | tf_op jit(solution)/shard_map/all_to_all | solution.py:96
  407.5 6.0 %fusion = bf16[64,8,3584]{2,1,0:T(8,128)(2,1)} fusion(f32[512,3584]{1,0:T(8,128)} %fusion.13, bf16[512,128]{0,1:T(8,128)(2,1)S(1)} %copy-done.1, bf16[1,3584,128]{2,1,0:T(8,128)(2,1)S(1)} %all-gather.1), kind=kOutput, calls=%fused_computation.2 | convolution fusion | flops 473432064 | bytes 12058624 | tf_op jit(solution)/shard_map/dot_general | solution.py:14
  413.5 7.2 %all-to-all-done.4 = bf16[64,1,8]{2,1,0:T(2,128)(2,1)S(1)} async-done(((bf16[64,1,8]{2,1,0:T(2,128)(2,1)}), bf16[64,1,8]{2,1,0:T(2,128)(2,1)S(1)}, u32[]{:S(2)}, u32[]{:S(2)}) %all-to-all-start.4) | async-done | bytes 1056 | tf_op jit(solution)/shard_map/all_to_all | solution.py:96
  420.7 7.9 %all-to-all-start.3 = ((bf16[64,8,3584]{2,1,0:T(8,128)(2,1)}), bf16[64,8,3584]{2,1,0:T(8,128)(2,1)}, u32[]{:S(2)}, u32[]{:S(2)}) async-start(bf16[64,8,3584]{2,1,0:T(8,128)(2,1)} %fusion), calls=%async_computation.3 | async-start | bytes 7340032 | tf_op jit(solution)/shard_map/all_to_all | solution.py:95
  428.7 3.0 convolution_convert_fusion.1
  431.7 3.2 convolution_convert_fusion
  435.0 2.7 copy.50
  439.1 42.3 %reduce-scatter.4.cloned.1.call-done = bf16[448,384]{1,0:T(8,128)(2,1)} async-done(((bf16[3584,384]{1,0:T(8,128)(2,1)}), bf16[448,384]{1,0:T(8,128)(2,1)}) %reduce-scatter.4.cloned.1.call-update) | async-done | bytes 344080
  481.4 1.0 fusion.33
  482.6 0.8 copy.46
  483.5 0.8 copy.47
  484.4 0.8 copy.48
  485.1 102.9 %all-to-all-done.3 = bf16[64,8,3584]{2,1,0:T(8,128)(2,1)} async-done(((bf16[64,8,3584]{2,1,0:T(8,128)(2,1)}), bf16[64,8,3584]{2,1,0:T(8,128)(2,1)}, u32[]{:S(2)}, u32[]{:S(2)}) %all-to-all-start.3) | async-done | bytes 3670048 | tf_op jit(solution)/shard_map/all_to_all | solution.py:95
  588.0 3.3 convolution_convert_fusion.4
  (46 shorter events, 4.8 us)
Async XLA Ops:
  7.2 22.9 %copy-start = (bf16[16,3584]{1,0:T(8,128)(2,1)S(1)}, bf16[16,3584]{1,0:T(8,128)(2,1)}, u32[]{:S(2)}) copy-start(bf16[16,3584]{1,0:T(8,128)(2,1)} %param.7) | copy-start | bytes 344068
  10.5 32.5 %all-to-all-start = ((bf16[64,1,8]{2,1,0:T(2,128)(2,1)}), bf16[64,1,8]{2,1,0:T(2,128)(2,1)S(1)}, u32[]{:S(2)}, u32[]{:S(2)}) async-start(bf16[64,1,8]{2,1,0:T(2,128)(2,1)} %copy.42), calls=%async_computation | async-start | bytes 65536 | tf_op jit(solution)/shard_map/all_to_all | solution.py:53
  45.0 5.7 copy-start.2
  45.1 165.1 %all-to-all-start.2 = ((bf16[64,8,3584]{2,1,0:T(8,128)(2,1)}), bf16[64,8,3584]{2,1,0:T(8,128)(2,1)}, u32[]{:S(2)}, u32[]{:S(2)}) async-start(bf16[64,8,3584]{2,1,0:T(8,128)(2,1)} %bitcast.61), calls=%async_computation.2 | async-start | bytes 7340032 | tf_op jit(solution)/shard_map/all_to_all | solution.py:51
  212.2 13.8 %copy-start.3 = (bf16[1,448,128]{2,1,0:T(8,128)(2,1)S(1)}, bf16[1,448,128]{2,1,0:T(8,128)(2,1)}, u32[]{:S(2)}) copy-start(bf16[1,448,128]{2,1,0:T(8,128)(2,1)} %param.11) | copy-start | bytes 344068
  212.2 28.6 %copy-start.4 = (bf16[1,448,128]{2,1,0:T(8,128)(2,1)S(1)}, bf16[1,448,128]{2,1,0:T(8,128)(2,1)}, u32[]{:S(2)}) copy-start(bf16[1,448,128]{2,1,0:T(8,128)(2,1)} %param.12) | copy-start | bytes 344068
  212.2 42.1 %copy-start.5 = (bf16[1,448,128]{2,1,0:T(8,128)(2,1)S(1)}, bf16[1,448,128]{2,1,0:T(8,128)(2,1)}, u32[]{:S(2)}) copy-start(bf16[1,448,128]{2,1,0:T(8,128)(2,1)} %param.13) | copy-start | bytes 344068
  212.2 172.8 %all-to-all-start.1 = ((bf16[64,8,3584]{2,1,0:T(8,128)(2,1)}), bf16[64,8,3584]{2,1,0:T(8,128)(2,1)}, u32[]{:S(2)}, u32[]{:S(2)}) async-start(bf16[64,8,3584]{2,1,0:T(8,128)(2,1)} %bitcast.60), calls=%async_computation.1 | async-start | bytes 7340032 | tf_op jit(solution)/shard_map/all_to_all | solution.py:52
  389.1 18.4 %copy-start.1 = (bf16[512,128]{0,1:T(8,128)(2,1)S(1)}, bf16[512,128]{0,1:T(8,128)(2,1)}, u32[]{:S(2)}) copy-start(bf16[512,128]{0,1:T(8,128)(2,1)} %get-tuple-element.33) | copy-start | bytes 393220
  394.0 26.8 %all-to-all-start.4 = ((bf16[64,1,8]{2,1,0:T(2,128)(2,1)}), bf16[64,1,8]{2,1,0:T(2,128)(2,1)S(1)}, u32[]{:S(2)}, u32[]{:S(2)}) async-start(bf16[64,1,8]{2,1,0:T(2,128)(2,1)} %convert_element_type.105), calls=%async_computation.4 | async-start | bytes 65536 | tf_op jit(solution)/shard_map/all_to_all | solution.py:96
  413.5 15.2 %copy-start.6 = (bf16[512,128]{0,1:T(8,128)(2,1)S(1)}, bf16[512,128]{0,1:T(8,128)(2,1)}, u32[]{:S(2)}) copy-start(bf16[512,128]{0,1:T(8,128)(2,1)} %get-tuple-element.31) | copy-start | bytes 393220
  420.7 167.3 %all-to-all-start.3 = ((bf16[64,8,3584]{2,1,0:T(8,128)(2,1)}), bf16[64,8,3584]{2,1,0:T(8,128)(2,1)}, u32[]{:S(2)}, u32[]{:S(2)}) async-start(bf16[64,8,3584]{2,1,0:T(8,128)(2,1)} %fusion), calls=%async_computation.3 | async-start | bytes 7340032 | tf_op jit(solution)/shard_map/all_to_all | solution.py:95
  428.7 52.8 %reduce-scatter.4.cloned.1.call-start = ((), (), s32[]{:S(2)}) async-start(), calls=%async_computation.6 | async-start | bytes 3096576
Sparse Core Ops, SparseCore 0:
  437.9 43.4 reduce-scatter.3
where the time goes:
time: 605 us; the launch traced here: 598 us
  waiting for transfers between devices  434 us (72%)
  starting transfers between devices  60.3 us (10%)
  blocking collectives  41.8 us (7%)
  matrix products  31.3 us (5%)
  local copies, waits for them, and re-layouts  14.9 us (2%)
  between operations  14.3 us (2%)
    all_to_all x1, waiting for transfers between devices, shards(): lax.all_to_all(send_x, 'expert', split_axis=0, concat_axis=0, tiled=True)  159 us
    all_to_all x1, waiting for transfers between devices, shards(): lax.all_to_all(send_dy, 'expert', split_axis=0, concat_axis=0, tiled=True)  110 us
    all_to_all x1, waiting for transfers between devices, shards(): lax.all_to_all(back_x, 'expert', split_axis=0, concat_axis=0, tiled=True)  103 us
    unnamed x2, waiting for transfers between devices  42.3 us
    all_to_all x1, starting transfers between devices, shards(): lax.all_to_all(send_p, 'expert', split_axis=0, concat_axis=0, tiled=True)  19.3 us
    dot_general x7, matrix products, mult(): return jnp.dot(left, right, preferred_element_type=jnp.float32)  15.1 us
    all_gather x1, blocking collectives, shards(): lax.all_gather(gate_rows, 'dp', axis=0, tiled=True)  14.8 us
    all_to_all x1, starting transfers between devices, shards(): lax.all_to_all(send_dy, 'expert', split_axis=0, concat_axis=0, tiled=True)  13.8 us
  transfers between devices with their start and end apart: 6, of which 6 were waited for; matrix products, arithmetic and copies ran while one was open for 5% of the time, Pallas kernels for 0%

commit v1 on v0

v1 whole, which is shorter than its diff:
```python
import jax
import jax.numpy as jnp
from jax import lax
from jax.sharding import PartitionSpec as P

NY = 4
NZ = 16
Z_GROUPS = [[y * NZ + z for z in range(NZ)] for y in range(NY)]
Y_GROUPS = [[y * NZ + z for y in range(NY)] for z in range(NZ)]


def mult(left, right, dims):
    return lax.dot_general(left, right, (dims, ((), ())), preferred_element_type=jnp.float32)


def shards(tokens, cotangent, expert_ids, gates, w_gate, w_up, w_down_t):
    bf = jnp.bfloat16
    half = lax.rem(lax.axis_index("expert"), NZ) // (NZ // 2)
    experts = jnp.arange(2 * NY, dtype=jnp.int32)
    hit = expert_ids[:, :, None] == experts[None, None, :]
    gate_mat = jnp.sum(jnp.where(hit, gates.astype(jnp.float32)[:, :, None], 0.0), axis=1).astype(bf)
    x = lax.all_gather(tokens, "expert", axis=0, tiled=True, axis_index_groups=Z_GROUPS)
    dy = lax.all_gather(cotangent, "expert", axis=0, tiled=True, axis_index_groups=Z_GROUPS)
    gm = lax.all_gather(gate_mat, "expert", axis=0, tiled=True, axis_index_groups=Z_GROUPS)
    w = jnp.concatenate([w_gate[0], w_up[0], w_down_t[0]], axis=1)
    w = lax.all_gather(w, "dp", axis=0, tiled=True)
    w = lax.all_gather(w, "expert", axis=0, tiled=False, axis_index_groups=Y_GROUPS)
    mine = jnp.where(half == 0, gm[:, 0::2], gm[:, 1::2]).astype(jnp.float32)
    total = 0.0
    parts = []
    grads = []
    for e in range(NY):
        pre = mult(x, w[e, :, :256], ((1,), (0,)))
        back = mult(dy, w[e, :, 256:], ((1,), (0,)))
        pre_gate, pre_up = pre[:, :128], pre[:, 128:]
        weight = mine[:, e : e + 1]
        sig = jax.nn.sigmoid(pre_gate)
        silu = pre_gate * sig
        hidden = silu * pre_up
        parts.append(jnp.sum(hidden * back, axis=1, keepdims=True))
        d_hidden = weight * back
        d_gate = d_hidden * pre_up * sig * (1.0 + pre_gate * (1.0 - sig))
        joined = jnp.concatenate([d_gate, d_hidden * silu], axis=1).astype(bf)
        total = total + mult(joined, w[e, :, :256], ((1,), (1,)))
        grads.append(
            jnp.concatenate(
                [
                    mult(x, joined, ((0,), (0,))),
                    mult(dy, (weight * hidden).astype(bf), ((0,), (0,))),
                ],
                axis=1,
            ).astype(bf)
        )
    part = jnp.concatenate(parts, axis=1)
    zero = jnp.zeros_like(part)
    part = jnp.where(half == 0, jnp.stack([part, zero], 2), jnp.stack([zero, part], 2)).reshape(-1, 2 * NY)
    grad_tokens = lax.psum_scatter(
        total.astype(bf), "expert", scatter_dimension=0, tiled=True, axis_index_groups=Z_GROUPS
    )
    part = lax.psum_scatter(part, "expert", scatter_dimension=0, tiled=True, axis_index_groups=Z_GROUPS)
    grad_gates = jnp.sum(jnp.where(hit, part[:, None, :], 0.0), axis=2)
    g = jnp.stack(grads)
    g = lax.psum_scatter(g, "expert", scatter_dimension=0, tiled=False, axis_index_groups=Y_GROUPS)
    g = lax.psum_scatter(g, "dp", scatter_dimension=0, tiled=True)
    return (grad_tokens, grad_gates, g[None, :, :128], g[None, :, 128:256], g[None, :, 256:])


def solution(mesh):
    row = P(("dp", "expert"), None)
    wide = P("expert", "dp", None)
    return jax.shard_map(
        shards,
        mesh=mesh,
        in_specs=(row, row, row, row, wide, wide, wide),
        out_specs=(row, row, wide, wide, wide),
        check_vma=False,
    )
```

time: 605 us -> 664 us (1.098)
  waiting for transfers between devices: 434 us -> 568 us
  starting transfers between devices: 60.3 us -> 0.5 us
  blocking collectives: 41.8 us -> 20.5 us
    all_to_all x5 -> x0, waiting for transfers between devices: 392 us -> none  [the longest x1 159 us: shards(): lax.all_to_all(send_x, 'expert', split_axis=0, concat_axis=0, tiled=True)]
    all_gather x0 -> x4, waiting for transfers between devices: none -> 284 us  [the longest x1 121 us: shards(): lax.all_gather(w, 'expert', axis=0, tiled=False, axis_index_groups=Y_GROUPS)]
    reduce_scatter x0 -> x2, waiting for transfers between devices: none -> 190 us  [the longest x1 127 us: shards(): lax.psum_scatter(g, 'expert', scatter_dimension=0, tiled=False, axis_inde...]
    all_to_all x5 -> x0, starting transfers between devices: 60.2 us -> none  [the longest x1 19.3 us: shards(): lax.all_to_all(send_p, 'expert', split_axis=0, concat_axis=0, tiled=True)]
    unnamed x2 -> x10, waiting for transfers between devices: 42.3 us -> 94.8 us
    all_gather x3 -> x1, blocking collectives: 41.8 us -> 20.5 us  [shards(): lax.all_gather(gate_mat, 'expert', axis=0, tiled=True, axis_index_groups=...]
    dot_general x11 -> x20, matrix products: 31.3 us -> 32.3 us  [mult(): lax.dot_general(left, right, (dims, ((), ())), preferred_element_type=jnp...]
  transfers between devices with their start and end apart: 6 -> 8, of which waited for: 6 -> 8; matrix products, arithmetic and copies ran while one was open for 5% -> 4% of each run, Pallas kernels for 0% -> 0%
where the time goes in v1:
time: 664 us; the launch traced here: 654 us
  waiting for transfers between devices  568 us (86%)
  matrix products  32.3 us (5%)
  blocking collectives  20.5 us (3%)
  between operations  14.4 us (2%)
  local copies, waits for them, and re-layouts  11.1 us (2%)
  other arithmetic  7.01 us (1%)
    reduce_scatter x1, waiting for transfers between devices, shards(): lax.psum_scatter(g, 'expert', scatter_dimension=0, tiled=False, axis_inde...  127 us
    all_gather x1, waiting for transfers between devices, shards(): lax.all_gather(w, 'expert', axis=0, tiled=False, axis_index_groups=Y_GROUPS)  121 us
    unnamed x10, waiting for transfers between devices  94.8 us
    all_gather x1, waiting for transfers between devices, shards(): lax.all_gather(tokens, 'expert', axis=0, tiled=True, axis_index_groups=Z_...  65.4 us
    reduce_scatter x1, waiting for transfers between devices, shards(): lax.psum_scatter(total.astype(bf), 'expert', scatter_dimension=0, tiled=T...  62.9 us
    all_gather x1, waiting for transfers between devices, shards(): lax.all_gather(cotangent, 'expert', axis=0, tiled=True, axis_index_groups...  57.3 us
    all_gather x1, waiting for transfers between devices, shards(): w = lax.all_gather(w, 'dp', axis=0, tiled=True)  40.1 us
    dot_general x20, matrix products, mult(): lax.dot_general(left, right, (dims, ((), ())), preferred_element_type=jnp...  32.3 us
  transfers between devices with their start and end apart: 8, of which 8 were waited for; matrix products, arithmetic and copies ran while one was open for 4% of the time, Pallas kernels for 0%

profile of v1, /device:TPU:1, one launch (start us, length us, event | category | flops | bytes accessed | tf_op | source)
XLA Modules:
  0.0 654.3 jit_solution(3658573188875909722)
XLA Ops:
  7.2 1.8 pad_maximum_fusion
  9.1 0.7 all-gather.11.cloned.1.call-update
  9.8 40.1 %all-gather.7.cloned.1.call-done = bf16[3584,384]{1,0:T(8,128)(2,1)} async-done(((bf16[448,384]{1,0:T(8,128)(2,1)}), bf16[3584,384]{1,0:T(8,128)(2,1)}) %all-gather.7.cloned.1.call-update) | async-done | bytes 2752528 | tf_op jit(solution)/shard_map/all_gather | solution.py:26
  50.6 65.4 %all-gather.11.cloned.1.call-done = bf16[256,3584]{1,0:T(8,128)(2,1)} async-done(((bf16[16,3584]{1,0:T(8,128)(2,1)}), bf16[256,3584]{1,0:T(8,128)(2,1)}) %all-gather.11.cloned.1.call-update) | async-done | bytes 1835024 | tf_op jit(solution)/shard_map/all_gather | solution.py:22
  116.0 121.2 %all-gather.13.cloned.1.call-done = bf16[14336,384]{1,0:T(8,128)(2,1)} async-done(((bf16[3584,384]{1,0:T(8,128)(2,1)}), bf16[14336,384]{1,0:T(8,128)(2,1)}) %all-gather.13.cloned.1.call-update) | async-done | bytes 11010064 | tf_op jit(solution)/shard_map/all_gather | solution.py:27
  237.2 2.9 fusion.17
  240.1 2.2 fusion.14
  242.3 2.2 fusion.15
  244.4 2.2 fusion.16
  246.6 57.3 %all-gather.9.cloned.1.call-done = bf16[256,3584]{1,0:T(8,128)(2,1)} async-done(((bf16[16,3584]{1,0:T(8,128)(2,1)}), bf16[256,3584]{1,0:T(8,128)(2,1)}) %all-gather.9.cloned.1.call-update) | async-done | bytes 1835024 | tf_op jit(solution)/shard_map/all_gather | solution.py:23
  303.9 2.6 multiply_reduce_fusion.3
  306.6 2.0 multiply_reduce_fusion
  308.6 1.9 multiply_reduce_fusion.1
  310.5 2.0 multiply_reduce_fusion.2
  312.6 0.8 copy.38
  313.5 63.3 %reduce-scatter.13.cloned.1.call-done = f32[16,8]{1,0:T(8,128)} async-done(((f32[256,8]{1,0:T(8,128)}), f32[16,8]{1,0:T(8,128)}) %reduce-scatter.13.cloned.1.call-update) | async-done | bytes 528
  376.8 0.8 copy.39
  378.1 20.5 %all-gather.1 = bf16[16,16,8]{1,2,0:T(8,128)(2,1)S(1)} all-gather(bf16[1,16,8]{1,2,0:T(8,128)(2,1)S(1)} %bitcast.162), channel_id=1, replica_groups={{0,1,2,3,4,5,6,7,8,9,10,11,12,13,14,15},{16,17,18,19,20,21,22,23,24,25,..., dimensions={0}, use_global_device_ids=true | all-gather | bytes 4352 | tf_op jit(solution)/shard_map/all_gather | solution.py:24
  399.2 1.1 copy-done.2
  404.6 4.3 maximum_maximum_fusion
  409.0 126.8 %reduce-scatter.11.cloned.1.call-done = bf16[1,3584,384]{1,2,0:T(8,128)(2,1)} async-done(((bf16[4,3584,384]{1,2,0:T(8,128)(2,1)}), bf16[1,3584,384]{1,2,0:T(8,128)(2,1)}) %reduce-scatter.11.cloned.1.call-update) | async-done | bytes 2752528 | tf_op jit(solution)/shard_map/reduce_scatter | solution.py:63
  535.8 4.5 copy.40
  540.5 2.2 fusion.9
  542.7 2.2 convolution_add_fusion.2
  545.0 2.2 convolution_add_fusion.1
  547.2 3.5 fusion
  550.7 30.2 %reduce-scatter.15.cloned.1.call-done = bf16[448,384]{1,0:T(8,128)(2,1)} async-done(((bf16[3584,384]{1,0:T(8,128)(2,1)}), bf16[448,384]{1,0:T(8,128)(2,1)}) %reduce-scatter.15.cloned.1.call-update) | async-done | bytes 344080
  580.9 1.0 fusion.38
  582.0 0.8 copy.35
  582.9 0.8 copy.36
  583.8 0.8 copy.37
  584.6 62.9 %reduce-scatter.9.cloned.1.call-done = bf16[16,3584]{1,0:T(8,128)(2,1)} async-done(((bf16[256,3584]{1,0:T(8,128)(2,1)}), bf16[16,3584]{1,0:T(8,128)(2,1)}) %reduce-scatter.9.cloned.1.call-update) | async-done | bytes 114704 | tf_op jit(solution)/shard_map/reduce_scatter | solution.py:57
  (51 shorter events, 6.8 us)
Async XLA Ops:
  7.2 42.7 %all-gather.7.cloned.1.call-start = ((), (), s32[]{:S(2)}) async-start(), calls=%async_computation.4 | async-start | bytes 3096576 | tf_op jit(solution)/shard_map/all_gather | solution.py:26
  9.0 107.0 %all-gather.11.cloned.1.call-start = ((), (), s32[]{:S(2)}) async-start(), calls=%async_computation.6 | async-start | bytes 1949696 | tf_op jit(solution)/shard_map/all_gather | solution.py:22
  9.8 227.4 %all-gather.13.cloned.1.call-start = ((), (), s32[]{:S(2)}) async-start(), calls=%async_computation.9 | async-start | bytes 13762560 | tf_op jit(solution)/shard_map/all_gather | solution.py:27
  49.9 254.0 %all-gather.9.cloned.1.call-start = ((), (), s32[]{:S(2)}) async-start(), calls=%async_computation.5 | async-start | bytes 1949696 | tf_op jit(solution)/shard_map/all_gather | solution.py:23
  50.5 326.3 %reduce-scatter.13.cloned.1.call-start = ((), (), s32[]{:S(2)}) async-start(), calls=%async_computation.10 | async-start | bytes 139264
  237.2 2.9 copy-start
  303.9 2.7 copy-start.1
  310.5 2.9 copy-start.4
  310.5 67.0 %copy-start.3 = (s32[16,2]{0,1:T(2,128)S(1)}, s32[16,2]{0,1:T(2,128)}, u32[]{:S(2)}) copy-start(s32[16,2]{0,1:T(2,128)} %param.9) | copy-start | bytes 388
  313.4 222.4 %reduce-scatter.11.cloned.1.call-start = ((), (), s32[]{:S(2)}) async-start(), calls=%async_computation.8 | async-start | bytes 13762560 | tf_op jit(solution)/shard_map/reduce_scatter | solution.py:63
  398.8 1.5 copy-start.2
  408.9 171.9 %reduce-scatter.15.cloned.1.call-start = ((), (), s32[]{:S(2)}) async-start(), calls=%async_computation.11 | async-start | bytes 3096576
  540.3 107.1 %reduce-scatter.9.cloned.1.call-start = ((), (), s32[]{:S(2)}) async-start(), calls=%async_computation.7 | async-start | bytes 1949696 | tf_op jit(solution)/shard_map/reduce_scatter | solution.py:57
Sparse Core Ops, SparseCore 0:
  10.1 39.7 all-gather.6
  52.0 63.9 all-gather.10
  118.1 119.0 all-gather.12
  239.1 64.7 all-gather.8
  313.5 63.2 reduce-scatter.12
  409.1 126.6 reduce-scatter.10
  540.4 40.4 reduce-scatter.14
  584.3 63.1 reduce-scatter.8

commit v2 on v1

v2 whole, which is shorter than its diff:
```python
import jax
import jax.numpy as jnp
from jax import lax
from jax.experimental import pallas as pl
from jax.experimental.pallas import tpu as pltpu
from jax.sharding import PartitionSpec as P

NX, NC, NY, NZ = 4, 2, 4, 16
ROWS = 16
D = 3584
LANES = 128
XW = D + LANES
CH = D // NX
QR = 112
FW = 384
C0 = 2 * CH
C1 = XW - C0
MESH = pl.DeviceIdType.MESH
BF = jnp.bfloat16
F32 = jnp.float32
N_SEM = 192


def dot(left, right, dims=((1,), (0,))):
    return lax.dot_general(left, right, (dims, ((), ())), preferred_element_type=F32)


def wrap(value, size):
    return lax.rem(value + size, size)


def kernel(tok, cot, gm, wg, wu, wd, dx_out, part_out, gg, gu, gd,
           xs, ys, w, xt, yt, joined, g, pair, dxa, dxb, rza, rzb,
           p1rel, p1fin, q1rel, q1fin, rel2, fin2, part_acc, ssem, rsem):
    dp = lax.axis_index("dp")
    ex = lax.axis_index("expert")
    x, c = lax.div(dp, NC), lax.rem(dp, NC)
    y, z = lax.div(ex, NZ), lax.rem(ex, NZ)
    half = lax.div(z, NZ // 2)
    other = 1 - c

    def dev(xx, cc, yy, zz):
        return (xx * NC + cc, yy * NZ + zz)

    x_next = (dev(wrap(x + 1, NX), c, y, z), dev(wrap(x - 1, NX), c, y, z))
    y_next = (dev(x, c, wrap(y + 1, NY), z), dev(x, c, wrap(y - 1, NY), z))
    z_next = (dev(x, c, y, wrap(z + 1, NZ)), dev(x, c, y, wrap(z - 1, NZ)))
    sibling = dev(x, other, y, z)

    barrier = pltpu.get_barrier_semaphore()
    for target in (*x_next, *y_next, *z_next, sibling):
        pl.semaphore_signal(barrier, inc=1, device_id=target, device_id_type=MESH)

    xs[z, :, :D] = tok[...]
    xs[z, :, D:] = gm[...]
    ys[z] = cot[...]
    w[y, x, c, :, :, 0:128] = wg[0].reshape(4, QR, 128)
    w[y, x, c, :, :, 128:256] = wu[0].reshape(4, QR, 128)
    w[y, x, c, :, :, 256:384] = wd[0].reshape(4, QR, 128)
    pl.semaphore_wait(barrier, 7)

    count = [0]
    pending = []

    def alloc(n=1):
        base = count[0]
        count[0] += n
        return base

    def xfer(src, dst, i, target):
        return pltpu.make_async_remote_copy(
            src_ref=src, dst_ref=dst, send_sem=ssem.at[i], recv_sem=rsem.at[i],
            device_id=target, device_id_type=MESH)

    def send(src, dst, i, target):
        copy = xfer(src, dst, i, target)
        copy.start()
        pending.append(copy)

    def recv(dst, i):
        xfer(dst, dst, i, sibling).wait_recv()

    z_sem = {(p, d, k): alloc() for p in (0, 1) for d in (0, 1) for k in range(8)}
    blocks = (xs, ys)

    def z_steps(p, d):
        return 8 if p == d else 7

    def z_block(p, d, k):
        return blocks[p].at[wrap(z - k if d == 0 else z + k, NZ)]

    def z_send(p, d, k):
        ref = z_block(p, d, k)
        send(ref, ref, z_sem[p, d, k], z_next[d])

    def z_step(k):
        for p in (0, 1):
            for d in (0, 1):
                if k <= z_steps(p, d):
                    recv(z_block(p, d, k), z_sem[p, d, k - 1])
                if k < z_steps(p, d):
                    z_send(p, d, k)

    first = (x, y)
    second = (y, x)
    first_next = (x_next, y_next)
    second_next = (y_next, x_next)
    shares = []

    def w_at(s, a, b, core, lo, n):
        if s == 0:
            return w.at[b, a, core, pl.ds(lo, n)]
        return w.at[a, b, core, pl.ds(2 + lo, n)]

    def share(s, a, b, lo=0, n=2):
        i = alloc()
        ref = w_at(s, a, b, c, lo, n)
        send(ref, ref, i, sibling)
        shares.append((w_at(s, a, b, other, lo, n), i))

    def pos(value, shift):
        return wrap(value + shift, 4)

    sem_a = {(s, d): alloc() for s in (0, 1) for d in (0, 1)}
    sem_ar = {(s, d): alloc() for s in (0, 1) for d in (0, 1)}
    sem_b = {(s, d, i): alloc() for s in (0, 1) for d in (0, 1) for i in range(4)}
    sem_br = {(s, d, i): alloc() for s in (0, 1) for d in (0, 1) for i in range(4)}
    SHIFT = (0, -1, 1, 2)

    def w_slot_send(s, i):
        a = pos(first[s], SHIFT[i])
        for d in (0, 1):
            ref = w_at(s, a, second[s], c, 0, 2)
            send(ref, ref, sem_b[s, d, i], second_next[s][d])

    def w_start():
        for s in (0, 1):
            for d in (0, 1):
                ref = w_at(s, first[s], second[s], c, 0, 2)
                send(ref, ref, sem_a[s, d], first_next[s][d])
        for s in (0, 1):
            w_slot_send(s, 0)
            share(s, first[s], second[s])

    def w_first():
        for s in (0, 1):
            for d in (0, 1):
                a = pos(first[s], -1 if d == 0 else 1)
                recv(w_at(s, a, second[s], c, 0, 2), sem_a[s, d])
                ref = w_at(s, a, second[s], c, d, 1)
                send(ref, ref, sem_ar[s, d], first_next[s][d])
        for s in (0, 1):
            w_slot_send(s, 1)
            w_slot_send(s, 2)
            share(s, pos(first[s], -1), second[s])
            share(s, pos(first[s], 1), second[s])

    def w_far():
        for s in (0, 1):
            a = pos(first[s], 2)
            for d in (0, 1):
                recv(w_at(s, a, second[s], c, d, 1), sem_ar[s, d])
            w_slot_send(s, 3)
            share(s, a, second[s])

    def w_slot(i):
        for s in (0, 1):
            a = pos(first[s], SHIFT[i])
            for d in (0, 1):
                b = pos(second[s], -1 if d == 0 else 1)
                recv(w_at(s, a, b, c, 0, 2), sem_b[s, d, i])
                ref = w_at(s, a, b, c, d, 1)
                send(ref, ref, sem_br[s, d, i], second_next[s][d])
                share(s, a, b)

    def w_slot_far(i):
        for s in (0, 1):
            a = pos(first[s], SHIFT[i])
            b = pos(second[s], 2)
            for d in (0, 1):
                recv(w_at(s, a, b, c, d, 1), sem_br[s, d, i])
            share(s, a, b)

    for d in (0, 1):
        z_send(0, d, 0)
    w_start()
    for d in (0, 1):
        z_send(1, d, 0)
    z_step(1)
    w_first()
    z_step(2)
    w_slot(0)
    w_far()
    z_step(3)
    w_slot_far(0)
    w_slot(1)
    z_step(4)
    w_slot_far(1)
    w_slot(2)
    z_step(5)
    w_slot_far(2)
    w_slot(3)
    z_step(6)
    w_slot_far(3)
    z_step(7)
    z_step(8)
    for ref, i in shares:
        recv(ref, i)

    def x_cols(ref, k):
        return ref[:, :, k * CH:(k + 1) * CH].reshape(NZ * ROWS, CH)

    for k in range(NX):
        xt[2 * k:2 * k + 2] = x_cols(xs, k).T.reshape(2, CH // 2, NZ * ROWS)
        yt[2 * k:2 * k + 2] = x_cols(ys, k).T.reshape(2, CH // 2, NZ * ROWS)

    part_acc[...] = jnp.zeros_like(part_acc)
    lane = lax.broadcasted_iota(jnp.int32, (NZ * ROWS, LANES), 1)
    order = tuple(pos(y, shift) for shift in (2, 1, -1, 0))
    pair_sem = alloc(4 * NX)

    def pair_copy(i, e, k):
        return xfer(g.at[e, k, other], pair.at[e, k], pair_sem + NX * i + k, sibling)

    def expert(i):
        e = order[i]
        pre = jnp.zeros((NZ * ROWS, 256), F32)
        back = jnp.zeros((NZ * ROWS, 128), F32)
        for k in range(NX):
            wk = w[e, k].reshape(CH, FW)
            pre = pre + dot(x_cols(xs, k), wk[:, :256])
            back = back + dot(x_cols(ys, k), wk[:, 256:])
        mine = lane == 2 * e + half
        gates = xs[:, :, D:].reshape(NZ * ROWS, LANES).astype(F32)
        weight = jnp.sum(jnp.where(mine, gates, 0.0), axis=1, keepdims=True)
        pre_gate, pre_up = pre[:, :128], pre[:, 128:]
        sig = 1.0 / (1.0 + jnp.exp(-pre_gate))
        silu = pre_gate * sig
        hidden = silu * pre_up
        part = jnp.sum(hidden * back, axis=1, keepdims=True)
        part_acc[...] += jnp.where(mine, part, 0.0)
        d_hidden = weight * back
        d_gate = d_hidden * pre_up * sig * (1.0 + pre_gate * (1.0 - sig))
        joined[i, :, :256] = jnp.concatenate([d_gate, d_hidden * silu], axis=1).astype(BF)
        joined[i, :, 256:] = (weight * hidden).astype(BF)

        def grads(k, core):
            row = 2 * k + core
            both = dot(xt[row], joined[i, :, :256])
            down = dot(yt[row], joined[i, :, 256:])
            return jnp.concatenate([both, down], axis=1).reshape(4, QR, FW)

        def away(k, carry):
            g[e, k, other] = grads(k, other).astype(BF)
            pair_copy(i, e, k).start()
            return carry

        def home(k, carry):
            own = grads(k, c)
            pair_copy(i, e, k).wait_recv()
            g[e, k, c] = (own + pair[e, k].astype(F32)).astype(BF)
            return carry

        lax.fori_loop(0, NX, away, 0)
        lax.fori_loop(0, NX, home, 0)

    def add(dst, *sources):
        total = dst[...].astype(F32)
        for source in sources:
            total = total + source[...].astype(F32)
        dst[...] = total.astype(BF)

    p1 = {name: alloc() for name in ("r0", "r1", "f0", "f1")}

    def p1_start():
        for d in (0, 1):
            send(g.at[order[0], :, c, d], p1rel.at[d], p1["r%d" % d], y_next[d])

    def p1_relay(d):
        e = order[1 + d]
        recv(p1rel.at[d], p1["r%d" % d])
        for k in range(NX):
            add(g.at[e, k, c, d], p1rel.at[d, k])
        send(g.at[e, :, c, pl.ds(0, 2)], p1fin.at[d], p1["f%d" % d], y_next[d])

    def p1_end():
        for d in (0, 1):
            recv(p1fin.at[d], p1["f%d" % d])
        for k in range(NX):
            add(g.at[y, k, c, pl.ds(0, 2)], p1fin.at[0, k], p1fin.at[1, k])

    class Ring:
        def __init__(self, at, nexts, relays, finals):
            self.at, self.nexts, self.relays, self.finals = at, nexts, relays, finals
            self.r = [alloc(), alloc()]
            self.f = [alloc(), alloc()]

        def start(self):
            for d in (0, 1):
                send(self.at(2, d, 1), self.relays.at[d], self.r[d], self.nexts[d])

        def relay(self, d):
            shift = 1 if d == 0 else -1
            recv(self.relays.at[d], self.r[d])
            add(self.at(shift, d, 1).at[0], self.relays.at[d, 0])
            send(self.at(shift, 0, 2), self.finals.at[d], self.f[d], self.nexts[d])

        def end(self):
            for d in (0, 1):
                recv(self.finals.at[d], self.f[d])
            add(self.at(0, 0, 2), self.finals.at[0], self.finals.at[1])

    p2 = Ring(lambda sh, lo, n: g.at[y, pos(x, sh), c, pl.ds(lo, n)], x_next, rel2.at[0], fin2.at[0])
    q1 = [
        Ring(lambda sh, lo, n, e=order[i]: g.at[e, pos(x, sh), c, pl.ds(2 + lo, n)], x_next, q1rel.at[i], q1fin.at[i])
        for i in range(NY)
    ]
    q2 = Ring(lambda sh, lo, n: g.at[pos(y, sh), x, c, pl.ds(2 + lo, n)], y_next, rel2.at[1], fin2.at[1])

    def both(ring):
        ring.relay(0)
        ring.relay(1)

    expert(0)
    p1_start()
    q1[0].start()
    expert(1)
    both(q1[0])
    q1[1].start()
    p1_relay(0)
    expert(2)
    q1[2].start()
    p1_relay(1)
    both(q1[1])
    expert(3)
    q1[3].start()

    def token_grads(k):
        total = jnp.zeros((NZ * ROWS, CH), F32)
        for i in range(NY):
            wk = w[order[i], k].reshape(CH, FW)
            total = total + dot(joined[i, :, :256], wk[:, :256], ((1,), (1,)))
        return total.astype(BF).reshape(NZ, ROWS, CH)

    acc = (dxa, dxb)
    land = (rza, rzb)
    back_sem = {(p, d, k): alloc() for p in (0, 1) for d in (0, 1) for k in range(8)}

    def back_target(p, d, k):
        n = z_steps(p, d)
        return wrap(z + n - k if d == 0 else z - n + k, NZ)

    def back_start(p):
        for d in (0, 1):
            send(acc[p].at[back_target(p, d, 0)], land[p].at[d, 0], back_sem[p, d, 0], z_next[d])

    def back_step(k):
        for p in (0, 1):
            for d in (0, 1):
                if k < z_steps(p, d):
                    here = land[p].at[d, k - 1]
                    recv(here, back_sem[p, d, k - 1])
                    add(here, acc[p].at[back_target(p, d, k)])
                    send(here, land[p].at[d, k], back_sem[p, d, k], z_next[d])

    dxa[:, :, :CH] = token_grads(0)
    dxa[:, :, CH:] = token_grads(1)
    back_start(0)
    dxb[:, :, :CH] = token_grads(2)
    dxb[:, :, CH:2 * CH] = token_grads(3)
    dxb[:, :, 2 * CH:] = part_acc[...].astype(BF).reshape(NZ, ROWS, LANES)
    back_start(1)

    q1[0].end()
    q2.start()
    back_step(1)
    both(q1[2])
    q1[1].end()
    q2.relay(0)
    back_step(2)
    p1_end()
    p2.start()
    back_step(3)
    both(q1[3])
    q1[2].end()
    q2.relay(1)
    back_step(4)
    both(p2)
    back_step(5)
    q1[3].end()
    q2.end()
    back_step(6)
    p2.end()
    back_step(7)

    def finish(p):
        total = acc[p][z].astype(F32)
        for d in (0, 1):
            k = z_steps(p, d) - 1
            recv(land[p].at[d, k], back_sem[p, d, k])
            total = total + land[p][d, k].astype(F32)
        return total

    dx_out[:, :C0] = finish(0).astype(BF)
    last = finish(1)
    dx_out[:, C0:] = last[:, :D - C0].astype(BF)
    part_out[...] = last[:, D - C0:]
    for s in (0, 1):
        res = g[y, x, c, 2 * s:2 * s + 2].reshape(2 * QR, FW)
        rows = slice(2 * QR * s, 2 * QR * (s + 1))
        gg[0, rows, :] = res[:, 0:128]
        gu[0, rows, :] = res[:, 128:256]
        gd[0, rows, :] = res[:, 256:384]

    for copy in pending:
        copy.wait_send()

    def drain(i):
        def body(k, carry):
            pair_copy(i, order[i], k).wait_send()
            return carry
        lax.fori_loop(0, NX, body, 0)

    for i in range(NY):
        drain(i)
    assert count[0] <= N_SEM, count[0]


def call(tok, cot, gm, wg, wu, wd):
    vm = pl.BlockSpec(memory_space=pltpu.VMEM)
    out = (
        jax.ShapeDtypeStruct((ROWS, D), BF),
        jax.ShapeDtypeStruct((ROWS, LANES), F32),
        *[jax.ShapeDtypeStruct((1, 448, 128), BF)] * 3,
    )
    scratch = [
        pltpu.VMEM((NZ, ROWS, XW), BF),
        pltpu.VMEM((NZ, ROWS, D), BF),
        pltpu.VMEM((NY, NX, NC, 4, QR, FW), BF),
        pltpu.VMEM((8, 448, 256), BF),
        pltpu.VMEM((8, 448, 256), BF),
        pltpu.VMEM((NY, NZ * ROWS, FW), BF),
        pltpu.VMEM((NY, NX, NC, 4, QR, FW), BF),
        pltpu.VMEM((NY, NX, 4, QR, FW), BF),
        pltpu.VMEM((NZ, ROWS, C0), BF),
        pltpu.VMEM((NZ, ROWS, C1), BF),
        pltpu.VMEM((2, 8, ROWS, C0), BF),
        pltpu.VMEM((2, 8, ROWS, C1), BF),
        pltpu.VMEM((2, NX, QR, FW), BF),
        pltpu.VMEM((2, NX, 2, QR, FW), BF),
        pltpu.VMEM((NY, 2, 1, QR, FW), BF),
        pltpu.VMEM((NY, 2, 2, QR, FW), BF),
        pltpu.VMEM((2, 2, 1, QR, FW), BF),
        pltpu.VMEM((2, 2, 2, QR, FW), BF),
        pltpu.VMEM((NZ * ROWS, LANES), F32),
        pltpu.SemaphoreType.DMA((N_SEM,)),
        pltpu.SemaphoreType.DMA((N_SEM,)),
    ]
    return pl.pallas_call(
        kernel,
        out_shape=out,
        in_specs=[vm] * 6,
        out_specs=(vm,) * 5,
        scratch_shapes=scratch,
        compiler_params=pltpu.CompilerParams(
            collective_id=0, has_side_effects=True, vmem_limit_bytes=60 * 1024 * 1024),
        cost_estimate=pl.CostEstimate(flops=7_600_000_000, bytes_accessed=2_000_000, transcendentals=131072),
    )(tok, cot, gm, wg, wu, wd)


def shards(tokens, cotangent, expert_ids, gates, w_gate, w_up, w_down_t):
    slots = jnp.arange(LANES, dtype=jnp.int32)
    hit = expert_ids[:, :, None] == slots[None, None, :]
    gm = jnp.sum(jnp.where(hit, gates.astype(F32)[:, :, None], 0.0), axis=1).astype(BF)
    grad_tokens, part, gg, gu, gd = call(tokens, cotangent, gm, w_gate, w_up, w_down_t)
    grad_gates = jnp.sum(jnp.where(hit, part[:, None, :], 0.0), axis=2)
    return grad_tokens, grad_gates, gg, gu, gd


def solution(mesh):
    row = P(("dp", "expert"), None)
    wide = P("expert", "dp", None)
    return jax.shard_map(
        shards,
        mesh=mesh,
        in_specs=(row, row, row, row, wide, wide, wide),
        out_specs=(row, row, wide, wide, wide),
        check_vma=False,
    )
```

time: 664 us -> 126 us (0.19)
  the two profiles are of different devices: /device:TPU:1 before, /device:TPU:8 now
where the time goes in v2:
time: 126 us
  Pallas kernels  118 us (94%)
  local copies, waits for them, and re-layouts  4.81 us (4%)
  other arithmetic  2.05 us (2%)
    pallas_call x1, Pallas kernels, call(): pl.pallas_call(kernel, out_shape=out, in_specs=[vm] * 6, out_specs=(vm,)...  118 us
    unnamed x14, local copies, waits for them, and re-layouts  4.81 us

profile of v2, /device:TPU:8, one launch (start us, length us, event | category | flops | bytes accessed | tf_op | source)
XLA Modules:
  0.0 125.6 jit_solution(1101458356554524855)
XLA Ops:
  0.6 0.0 copy-start.4
  0.6 0.7 convert_element_type.6
  1.3 0.0 copy-done.4
  1.3 0.7 select_reduce_fusion.1.gm
  2.0 118.1 %shard_map.110 = (bf16[16,3584]{1,0:T(8,128)(2,1)}, f32[16,128]{1,0:T(8,128)}, bf16[1,448,128]{2,1,0:T(8,128)(2,1)}, bf16[1,448,128]{2,1,0:T(8,128)(2,1)}, bf16[1,448,128]{2,1,0:T(8,128)(2,1)}) custom-call(bf16[16,3584]{1,0:T(8,128)(2,1)} %tok.1, bf16[16,3584]{1,0:T(8,128)(2,1)} %cot.1, bf16[16,128]{1,0:T(8,128)(2,1)} %select_reduce_fusion.1.gm, ...), custom_call_target="tpu_custom_call" | custom-call | flops 7600000000 | bytes 2000000 | tf_op jit(solution)/shard_map/pallas_call | solution.py:459
  120.1 0.0 copy-start.3
  120.1 0.7 copy-done.3
  120.8 0.7 select_reduce_fusion
  121.5 0.0 copy-start.2
  121.5 1.6 %copy.18 = bf16[16,3584]{1,0:T(8,128)(2,1)} copy(bf16[16,3584]{1,0:T(8,128)(2,1)} %get-tuple-element.20) | data formatting | bytes 229376
  123.1 0.0 copy-done.2
  123.1 0.0 copy-start.1
  123.1 0.6 copy.19
  123.7 0.3 copy-done.1
  124.0 0.0 copy-start
  124.0 0.6 copy.20
  124.7 0.3 copy-done
  124.9 0.6 copy.21
Async XLA Ops:
  0.6 0.7 copy-start.4
  120.1 0.7 copy-start.3
  121.5 1.6 %copy-start.2 = (bf16[1,448,128]{2,1,0:T(8,128)(2,1)S(1)}, bf16[1,448,128]{2,1,0:T(8,128)(2,1)}, u32[]{:S(2)}) copy-start(bf16[1,448,128]{2,1,0:T(8,128)(2,1)} %get-tuple-element.22) | copy-start | bytes 344068
  123.1 0.9 copy-start.1
  124.0 0.9 copy-start

commit v3 on v1

v3 whole, which is shorter than its diff:
```python
import jax
import jax.numpy as jnp
from jax import lax
from jax.experimental import pallas as pl
from jax.experimental.pallas import tpu as pltpu
from jax.sharding import PartitionSpec as P

NX, NC, NY, NZ = 4, 2, 4, 16
ROWS = 16
PAIR = NC * ROWS
D = 3584
LANES = 128
DH = D // NC
XW = DH + LANES
PIECE = DH // NX
TOK = NZ * PAIR
CHUNKS = ((0, 8), (8, 4), (12, 4))
PARTS = ((0, 0, 1024), (0, 1024, 896), (1, 0, 896), (1, 896, 896))
HOME = ((0, 896), (896, 1024))
QR = 112
FW = 384
TILE = 256
MESH = pl.DeviceIdType.MESH
BF = jnp.bfloat16
F32 = jnp.float32
N_SEM = 320

ORDER = (
    ("fy", 0), ("fx", 0), ("el", 2, 1), ("el", 3, 1), ("fx", 2), ("fx", 3), ("ty",), ("tx",), ("fx", 1), ("fy", 2),
    ("el", 0, 2), ("dw", 0), ("q10", "s"), ("p10", "s"), ("p12", "s"), ("p11", "s"), ("el", 1, 2), ("dw", 1),
    ("q11", "s"), ("el", 2, 2), ("dw", 2), ("p10", "r", 1), ("q12", "s"), ("p10", "r", 0), ("q10", "r", 0),
    ("p12", "r", 1), ("q11", "r", 1), ("p12", "r", 0), ("q11", "r", 0), ("q10", "r", 1), ("el", 3, 2), ("dx", 1),
    ("hs", 1), ("p11", "r", 1), ("dx", 0), ("hs", 0), ("dw", 3), ("h", 1, 1, 1, 1), ("h", 1, 0, 0, 1),
    ("h", 0, 1, 0, 1), ("h", 0, 1, 1, 1), ("q13", "s"), ("h", 1, 1, 0, 1), ("h", 1, 0, 1, 1), ("p10", "e"),
    ("p2", "s"), ("h", 0, 0, 0, 1), ("p11", "r", 0), ("h", 1, 1, 1, 2), ("h", 0, 0, 1, 1), ("h", 1, 0, 0, 2),
    ("q12", "r", 0), ("h", 0, 1, 1, 2), ("h", 0, 1, 0, 2), ("p13", "s"), ("q12", "r", 1), ("h", 1, 0, 1, 2),
    ("h", 1, 1, 0, 2), ("h", 1, 1, 1, 3), ("p12", "e"), ("h", 0, 0, 0, 2), ("h", 0, 0, 1, 2), ("q11", "e"),
    ("h", 1, 0, 0, 3), ("h", 0, 1, 1, 3), ("q10", "e"), ("h", 0, 1, 0, 3), ("h", 1, 0, 1, 3), ("h", 1, 1, 0, 3),
    ("q2", "s"), ("q13", "r", 0), ("q13", "r", 1), ("h", 1, 1, 1, 4), ("h", 0, 0, 1, 3), ("h", 0, 0, 0, 3),
    ("h", 1, 0, 0, 4), ("p11", "e"), ("h", 0, 1, 1, 4), ("h", 0, 1, 0, 4), ("p2", "r", 1), ("h", 1, 0, 1, 4),
    ("p2", "r", 0), ("h", 1, 1, 1, 5), ("h", 0, 0, 0, 4), ("h", 1, 1, 0, 4), ("p13", "r", 0), ("h", 0, 0, 1, 4),
    ("p13", "r", 1), ("h", 1, 0, 0, 5), ("h", 0, 1, 1, 5), ("h", 0, 1, 0, 5), ("h", 1, 0, 1, 5), ("h", 0, 0, 0, 5),
    ("q2", "r", 0), ("h", 1, 1, 1, 6), ("h", 1, 1, 0, 5), ("q12", "e"), ("q2", "r", 1), ("h", 1, 0, 0, 6),
    ("h", 0, 0, 1, 5), ("h", 0, 1, 1, 6), ("h", 0, 1, 0, 6), ("h", 1, 0, 1, 6), ("h", 0, 0, 0, 6),
    ("h", 1, 1, 1, 7), ("h", 1, 1, 0, 6), ("h", 0, 0, 1, 6), ("h", 1, 0, 0, 7), ("p13", "e"), ("h", 0, 1, 1, 7),
    ("q13", "e"), ("h", 0, 0, 0, 7), ("l1",), ("l0",), ("q2", "e"), ("p2", "e"),
)


def dot(left, right, dims=((1,), (0,))):
    return lax.dot_general(left, right, (dims, ((), ())), preferred_element_type=F32)


def wrap(value, size):
    return lax.rem(value + size, size)


def kernel(tok, cot, ids, gates, wg, wu, wd, dx_out, part_out, gw,
           xs, ys, stage, w, xt, yt, pre_s, pre_r, back_s, back_r, joined, g, dxs, land,
           q1rel, q1fin, p1rel, p1fin, rel2, fin2, part_acc, fin, leave, ssem, rsem):
    dp = lax.axis_index("dp")
    ex = lax.axis_index("expert")
    x, c = lax.div(dp, NC), lax.rem(dp, NC)
    y, z = lax.div(ex, NZ), lax.rem(ex, NZ)
    half = lax.div(z, NZ // 2)
    other = 1 - c

    def dev(xx, cc, yy, zz):
        return (xx * NC + cc, yy * NZ + zz)

    x_next = (dev(wrap(x + 1, NX), c, y, z), dev(wrap(x - 1, NX), c, y, z))
    y_next = (dev(x, c, wrap(y + 1, NY), z), dev(x, c, wrap(y - 1, NY), z))
    z_next = (dev(x, c, y, wrap(z + 1, NZ)), dev(x, c, y, wrap(z - 1, NZ)))
    sibling = dev(x, other, y, z)

    barrier = pltpu.get_barrier_semaphore()
    for target in (*x_next, *y_next, *z_next, sibling):
        pl.semaphore_signal(barrier, inc=1, device_id=target, device_id_type=MESH)

    count = [0]
    pending = []

    def alloc(n=1):
        base = count[0]
        count[0] += n
        return base

    def xfer(src, dst, i, target):
        return pltpu.make_async_remote_copy(
            src_ref=src, dst_ref=dst, send_sem=ssem.at[i], recv_sem=rsem.at[i],
            device_id=target, device_id_type=MESH)

    def send(src, dst, i, target):
        copy = xfer(src, dst, i, target)
        copy.start()
        pending.append(copy)

    def recv(dst, i):
        xfer(dst, dst, i, sibling).wait_recv()

    own = pl.ds(pl.multiple_of(c * ROWS, ROWS), ROWS)
    sib = pl.ds(pl.multiple_of(other * ROWS, ROWS), ROWS)
    row_of = (own, sib)

    def split(ref):
        value = ref[...].astype(F32)
        return [
            jnp.concatenate([value[:, PIECE * (2 * k + h):PIECE * (2 * k + h + 1)] for k in range(NX)], axis=1)
            for h in range(NC)
        ]

    w[y, x, :, :, 0:128] = wg[0].reshape(4, QR, 128)
    w[y, x, :, :, 128:256] = wu[0].reshape(4, QR, 128)
    w[y, x, :, :, 256:384] = wd[0].reshape(4, QR, 128)
    slot_ids = lax.broadcasted_iota(jnp.int32, (LANES, ROWS), 0)
    hits = [slot_ids == ids[k:k + 1, :] for k in range(2)]
    gates_t = gates[...].astype(F32)
    gate_mat = sum(jnp.where(hits[k], gates_t[k:k + 1, :], 0.0) for k in range(2)).T.astype(BF)
    for n, (src, dst) in enumerate(((tok, xs), (cot, ys))):
        low, high = split(src)
        dst[0, own, :DH] = jnp.where(c == 0, low, high).astype(BF)
        stage[n] = jnp.where(c == 0, high, low).astype(BF)
    xs[0, own, DH:] = gate_mat
    pl.semaphore_wait(barrier, 7)

    arrays = (xs, ys)
    z_sem = {(n, p, d, k): alloc() for n in range(len(PARTS)) for p in (0, 1) for d in (0, 1) for k in range(8)}
    stage_sem = [alloc(), alloc()]
    gate_sem = [alloc() for _ in CHUNKS]

    def z_steps(p, d):
        return 8 if p == d else 7

    def slot(d, k):
        if k in (0, 8):
            return 0 if k == 0 else NZ - 1
        return 2 * k - 1 + d

    def z_ref(n, p, d, k):
        a, lo, size = PARTS[n]
        size = min(size, DH - lo) if p == 1 else size
        return arrays[a].at[slot(d, k), row_of[p], pl.ds(lo, size)]

    def z_send(n, p, d, k):
        send(z_ref(n, p, d, k), z_ref(n, p, d, k + 1), z_sem[n, p, d, k], z_next[d])

    def stage_send(n):
        if n == 0:
            send(stage.at[0], xs.at[0, own, pl.ds(0, DH)], stage_sem[0], sibling)
        else:
            send(stage.at[1], ys.at[0, own], stage_sem[1], sibling)

    def stage_recv(n):
        recv(arrays[n].at[0, sib, pl.ds(0, DH)], stage_sem[n])

    def gate_part(h, which):
        lo, n = CHUNKS[h]
        return xs.at[lo:lo + n, which, pl.ds(DH, LANES)]

    def gate_share(h):
        send(gate_part(h, own), gate_part(h, own), gate_sem[h], sibling)

    def gate_recv(h):
        recv(gate_part(h, sib), gate_sem[h])

    def z_begin(p, a):
        for n in range(len(PARTS)):
            if PARTS[n][0] == a:
                for d in (0, 1):
                    z_send(n, p, d, 0)

    def z_one(n, p, k):
        for d in (0, 1):
            if k <= z_steps(p, d):
                recv(z_ref(n, p, d, k), z_sem[n, p, d, k - 1])
            if k < z_steps(p, d):
                z_send(n, p, d, k)

    def z_step(k, between=()):
        jobs = list(between)
        for p in (0, 1):
            for n in range(len(PARTS)):
                z_one(n, p, k)
                if jobs:
                    jobs.pop(0)()
        for job in jobs:
            job()

    first = (x, y)
    second = (y, x)
    first_next = (x_next, y_next)
    second_next = (y_next, x_next)

    def w_at(s, a, b, lo, n):
        if s == 0:
            return w.at[b, a, pl.ds(lo, n)]
        return w.at[a, b, pl.ds(2 + lo, n)]

    def pos(value, shift):
        return wrap(value + shift, 4)

    sem_a = {(s, d): alloc() for s in (0, 1) for d in (0, 1)}
    sem_ar = {(s, d): alloc() for s in (0, 1) for d in (0, 1)}
    sem_b = {(s, d, i): alloc() for s in (0, 1) for d in (0, 1) for i in range(4)}
    sem_br = {(s, d, i): alloc() for s in (0, 1) for d in (0, 1) for i in range(4)}
    SHIFT = (0, -1, 1, 2)

    def w_slot_send(s, i):
        a = pos(first[s], SHIFT[i])
        for d in (0, 1):
            ref = w_at(s, a, second[s], 0, 2)
            send(ref, ref, sem_b[s, d, i], second_next[s][d])

    def w_start():
        for s in (0, 1):
            for d in (0, 1):
                ref = w_at(s, first[s], second[s], 0, 2)
                send(ref, ref, sem_a[s, d], first_next[s][d])
        for s in (0, 1):
            w_slot_send(s, 0)

    def w_first():
        for s in (0, 1):
            for d in (0, 1):
                a = pos(first[s], -1 if d == 0 else 1)
                recv(w_at(s, a, second[s], 0, 2), sem_a[s, d])
                ref = w_at(s, a, second[s], d, 1)
                send(ref, ref, sem_ar[s, d], first_next[s][d])
        for s in (0, 1):
            w_slot_send(s, 1)
            w_slot_send(s, 2)

    def w_far():
        for s in (0, 1):
            a = pos(first[s], 2)
            for d in (0, 1):
                recv(w_at(s, a, second[s], d, 1), sem_ar[s, d])
            w_slot_send(s, 3)

    def w_slot(i):
        for s in (0, 1):
            a = pos(first[s], SHIFT[i])
            for d in (0, 1):
                b = pos(second[s], -1 if d == 0 else 1)
                recv(w_at(s, a, b, 0, 2), sem_b[s, d, i])
                ref = w_at(s, a, b, d, 1)
                send(ref, ref, sem_br[s, d, i], second_next[s][d])

    def w_slot_far(i):
        for s in (0, 1):
            a = pos(first[s], SHIFT[i])
            b = pos(second[s], 2)
            for d in (0, 1):
                recv(w_at(s, a, b, d, 1), sem_br[s, d, i])

    order = tuple(pos(y, shift) for shift in (2, 1, -1, 0))
    pre_sem = {(i, h): alloc() for i in range(NY) for h in range(len(CHUNKS))}
    back_sem = {(i, h): alloc() for i in (0, 2) for h in range(len(CHUNKS))}

    def rows(ref, h, lanes):
        lo, n = CHUNKS[h]
        return ref[lo:lo + n, :, lanes].reshape(n * PAIR, -1)

    def span(h):
        lo, n = CHUNKS[h]
        return pl.ds(PAIR * lo, PAIR * n)

    def weights(i, lanes):
        return w[order[i], :, :, :, lanes].reshape(DH, -1)

    def transpose(src, dst, h):
        lo, n = CHUNKS[h]

        def body(j, carry):
            at = pl.ds(pl.multiple_of(j * TILE, TILE), TILE)
            dst[at, span(h)] = src[lo:lo + n, :, at].reshape(n * PAIR, TILE).T
            return carry
        lax.fori_loop(0, DH // TILE, body, 0)

    def pre_copy(i, h):
        return pre_s.at[i, span(h)], pre_r.at[i, span(h)], pre_sem[i, h]

    def back_copy(i, h):
        at = (span(h), pl.ds(128 * i, 256))
        return back_s.at[at], back_r.at[at], back_sem[i, h]

    def fwd_x(i, h):
        pre_s[i, span(h), :] = dot(rows(xs, h, slice(0, DH)), weights(i, slice(0, 256)))
        send(*pre_copy(i, h), sibling)

    def fwd_y(i, h):
        both = jnp.concatenate([weights(i, slice(256, 384)), weights(i + 1, slice(256, 384))], axis=1)
        back_s[span(h), 128 * i:128 * (i + 2)] = dot(rows(ys, h, slice(0, DH)), both)
        send(*back_copy(i, h), sibling)

    def elementwise(i, h):
        e = order[i]
        n = CHUNKS[h][1]
        if i == 0:
            gate_recv(h)
        recv(*pre_copy(i, h)[1:])
        if i % 2 == 0:
            recv(*back_copy(i, h)[1:])
        mine = lax.broadcasted_iota(jnp.int32, (n * PAIR, LANES), 1) == 2 * e + half
        pre = pre_s[i, span(h), :] + pre_r[i, span(h), :]
        back = back_s[span(h), 128 * i:128 * (i + 1)] + back_r[span(h), 128 * i:128 * (i + 1)]
        gate = rows(xs, h, slice(DH, XW)).astype(F32)
        weight = jnp.sum(jnp.where(mine, gate, 0.0), axis=1, keepdims=True)
        pre_gate, pre_up = pre[:, :128], pre[:, 128:]
        sig = 1.0 / (1.0 + jnp.exp(-pre_gate))
        silu = pre_gate * sig
        hidden = silu * pre_up
        part = jnp.where(mine, jnp.sum(hidden * back, axis=1, keepdims=True), 0.0)
        part_acc[span(h), :] = part if i == 0 else part_acc[span(h), :] + part
        d_hidden = weight * back
        d_gate = d_hidden * pre_up * sig * (1.0 + pre_gate * (1.0 - sig))
        joined[i, span(h), 0:128] = d_gate.astype(BF)
        joined[i, span(h), 128:256] = (d_hidden * silu).astype(BF)
        joined[i, span(h), 256:384] = (weight * hidden).astype(BF)

    def weight_grads(i):
        e = order[i]

        def body(k, carry):
            at = pl.ds(pl.multiple_of(k * PIECE, PIECE), PIECE)
            g[e, k, :, :, 0:256] = dot(xt[at, :], joined[i, :, 0:256]).astype(BF).reshape(4, QR, 256)
            g[e, k, :, :, 256:384] = dot(yt[at, :], joined[i, :, 256:384]).astype(BF).reshape(4, QR, 128)
            return carry
        lax.fori_loop(0, NX, body, 0)

    def token_grads(k, lo):
        at = pl.ds(lo * PAIR, NZ // 2 * PAIR)
        total = jnp.zeros((NZ // 2 * PAIR, DH // 2), F32)
        for i in range(NY):
            wk = w[order[i], 2 * k:2 * k + 2, :, :, 0:256].reshape(DH // 2, 256)
            total = total + dot(joined[i, at, 0:256], wk, ((1,), (1,)))
        dxs[lo:lo + NZ // 2, :, k * (DH // 2):(k + 1) * (DH // 2)] = (
            total.astype(BF).reshape(NZ // 2, PAIR, DH // 2))
        if k == 1:
            dxs[lo:lo + NZ // 2, :, DH:] = part_acc[at, :].astype(BF).reshape(NZ // 2, PAIR, LANES)

    def later(fn, *args):
        return lambda: fn(*args)

    stage_send(0)
    z_begin(0, 0)
    w_start()
    stage_send(1)
    z_begin(0, 1)
    stage_recv(0)
    z_begin(1, 0)
    stage_recv(1)
    z_begin(1, 1)
    w_first()
    z_step(1)
    w_slot(0)
    w_far()
    z_step(2)
    w_slot(1)
    z_step(3)
    w_slot(2)
    w_slot_far(0)
    z_step(4)
    w_slot(3)
    w_slot_far(1)
    gate_share(0)
    z_step(5, [later(transpose, xs, xt, 0), later(transpose, ys, yt, 0)])
    w_slot_far(2)
    w_slot_far(3)
    z_step(6, [later(fwd_x, i, 0) for i in range(NY)] + [later(fwd_y, 0, 0), later(fwd_y, 2, 0)])
    gate_share(1)
    z_step(7, [job for i in range(NY) for job in (later(elementwise, i, 0), later(fwd_x, i, 1))])
    z_step(8, [
        later(fwd_y, 0, 1), later(fwd_y, 2, 1), later(transpose, xs, xt, 1), later(transpose, ys, yt, 1),
        later(token_grads, 0, 0), later(token_grads, 1, 0), later(elementwise, 0, 1), later(elementwise, 1, 1)])
    gate_share(2)

    def add(dst, *sources):
        total = dst[...].astype(F32)
        for source in sources:
            total = total + source[...].astype(F32)
        dst[...] = total.astype(BF)

    class Ring:
        def __init__(self, at, nexts, relays, finals):
            self.at, self.nexts, self.relays, self.finals = at, nexts, relays, finals
            self.r = [alloc(), alloc()]
            self.f = [alloc(), alloc()]

        def start(self):
            for d in (0, 1):
                send(self.at(2, d, 1), self.relays.at[d], self.r[d], self.nexts[d])

        def relay(self, d):
            shift = 1 if d == 0 else -1
            recv(self.relays.at[d], self.r[d])
            add(self.at(shift, d, 1), self.relays.at[d])
            send(self.at(shift, 0, 2), self.finals.at[d], self.f[d], self.nexts[d])

        def end(self):
            for d in (0, 1):
                recv(self.finals.at[d], self.f[d])
            add(self.at(0, 0, 2), self.finals.at[0], self.finals.at[1])

    order_x = tuple(pos(x, shift) for shift in (2, 1, -1, 0))
    p1 = [
        Ring(lambda sh, lo, n, a=order_x[i]: g.at[pos(y, sh), a, pl.ds(lo, n)], y_next, p1rel.at[i], p1fin.at[i])
        for i in range(NX)
    ]
    q1 = [
        Ring(lambda sh, lo, n, e=order[i]: g.at[e, pos(x, sh), pl.ds(2 + lo, n)], x_next, q1rel.at[i], q1fin.at[i])
        for i in range(NY)
    ]
    p2 = Ring(lambda sh, lo, n: g.at[y, pos(x, sh), pl.ds(lo, n)], x_next, rel2.at[0], fin2.at[0])
    q2 = Ring(lambda sh, lo, n: g.at[pos(y, sh), x, pl.ds(2 + lo, n)], y_next, rel2.at[1], fin2.at[1])

    home_sem = {(p, m, d, k): alloc() for p in (0, 1) for m in (0, 1) for d in (0, 1) for k in range(8)}
    fin_sem = alloc()

    def home_lanes(p, m):
        lo, size = HOME[m]
        return pl.ds(lo, min(size, DH - lo) if p == 1 else size)

    def home_src(p, m, d, k):
        return dxs.at[slot(1 - d, z_steps(p, d) - k), row_of[p], home_lanes(p, m)]

    def home_land(p, m, d, k):
        return land.at[p, d, k, :, home_lanes(p, m)]

    def home_start(m):
        for p in (1, 0):
            for d in (0, 1):
                send(home_src(p, m, d, 0), home_land(p, m, d, 0), home_sem[p, m, d, 0], z_next[d])

    def home_step(m, p, d, k):
        here = home_land(p, m, d, k - 1)
        recv(here, home_sem[p, m, d, k - 1])
        add(here, home_src(p, m, d, k))
        send(here, home_land(p, m, d, k), home_sem[p, m, d, k], z_next[d])

    def home_last(p):
        lanes = slice(0, DH if p == 1 else XW)
        total = dxs[0, row_of[p], lanes].astype(F32)
        for d in (0, 1):
            k = z_steps(p, d) - 1
            for m in (0, 1):
                recv(home_land(p, m, d, k), home_sem[p, m, d, k])
            total = total + land[p, d, k, :, lanes].astype(F32)
        return total

    def last_sibling():
        leave[...] = home_last(1).astype(BF)
        send(leave, fin.at[c], fin_sem, sibling)

    def last_own():
        mine = home_last(0)
        fin[c] = mine[:, :DH].astype(BF)
        part = mine[:, DH:].T
        part_out[...] = jnp.concatenate(
            [jnp.sum(jnp.where(hits[k], part, 0.0), axis=0, keepdims=True) for k in range(2)], axis=0)

    jobs = {
        "fx": lambda i: fwd_x(i, 2),
        "fy": lambda i: fwd_y(i, 2),
        "tx": lambda: transpose(xs, xt, 2),
        "ty": lambda: transpose(ys, yt, 2),
        "el": elementwise,
        "dw": weight_grads,
        "dx": lambda m: token_grads(m, NZ // 2),
        "hs": home_start,
        "h": home_step,
        "l1": last_sibling,
        "l0": last_own,
    }
    rings = {"p1%d" % i: ring for i, ring in enumerate(p1)}
    rings.update({"q1%d" % i: ring for i, ring in enumerate(q1)})
    rings.update({"p2": p2, "q2": q2})
    for name, *rest in ORDER:
        if name in rings:
            {"s": rings[name].start, "r": rings[name].relay, "e": rings[name].end}[rest[0]](*rest[1:])
        else:
            jobs[name](*rest)

    gw[...] = g[y, x].reshape(4 * QR, FW)
    recv(fin.at[other], fin_sem)
    low, high = fin[0].astype(F32), fin[1].astype(F32)
    dx_out[...] = jnp.concatenate(
        [part[:, PIECE * k:PIECE * (k + 1)] for k in range(NX) for part in (low, high)], axis=1).astype(BF)

    for copy in pending:
        copy.wait_send()
    assert count[0] <= N_SEM, count[0]


def call(tok, cot, ids, gates, wg, wu, wd):
    vm = pl.BlockSpec(memory_space=pltpu.VMEM)
    out = (
        jax.ShapeDtypeStruct((ROWS, D), BF),
        jax.ShapeDtypeStruct((2, ROWS), F32),
        jax.ShapeDtypeStruct((4 * QR, FW), BF),
    )
    scratch = [
        pltpu.VMEM((NZ, PAIR, XW), BF),
        pltpu.VMEM((NZ, PAIR, DH), BF),
        pltpu.VMEM((2, ROWS, DH), BF),
        pltpu.VMEM((NY, NX, 4, QR, FW), BF),
        pltpu.VMEM((DH, TOK), BF),
        pltpu.VMEM((DH, TOK), BF),
        pltpu.VMEM((NY, TOK, 256), F32),
        pltpu.VMEM((NY, TOK, 256), F32),
        pltpu.VMEM((TOK, 512), F32),
        pltpu.VMEM((TOK, 512), F32),
        pltpu.VMEM((NY, TOK, FW), BF),
        pltpu.VMEM((NY, NX, 4, QR, FW), BF),
        pltpu.VMEM((NZ, PAIR, XW), BF),
        pltpu.VMEM((2, 2, 8, ROWS, XW), BF),
        pltpu.VMEM((NY, 2, 1, QR, FW), BF),
        pltpu.VMEM((NY, 2, 2, QR, FW), BF),
        pltpu.VMEM((NX, 2, 1, QR, FW), BF),
        pltpu.VMEM((NX, 2, 2, QR, FW), BF),
        pltpu.VMEM((2, 2, 1, QR, FW), BF),
        pltpu.VMEM((2, 2, 2, QR, FW), BF),
        pltpu.VMEM((TOK, LANES), F32),
        pltpu.VMEM((NC, ROWS, DH), BF),
        pltpu.VMEM((ROWS, DH), BF),
        pltpu.SemaphoreType.DMA((N_SEM,)),
        pltpu.SemaphoreType.DMA((N_SEM,)),
    ]
    return pl.pallas_call(
        kernel,
        out_shape=out,
        in_specs=[vm] * 7,
        out_specs=(vm,) * 3,
        scratch_shapes=scratch,
        compiler_params=pltpu.CompilerParams(
            collective_id=0, has_side_effects=True, vmem_limit_bytes=60 * 1024 * 1024),
        cost_estimate=pl.CostEstimate(flops=7_600_000_000, bytes_accessed=2_000_000, transcendentals=262144),
    )(tok, cot, ids, gates, wg, wu, wd)


def shards(tokens, cotangent, expert_ids, gates, w_gate, w_up, w_down_t):
    grad_tokens, grad_gates, gw = call(
        tokens, cotangent, expert_ids.T, gates.T, w_gate, w_up, w_down_t)
    return grad_tokens, grad_gates.T, gw[None, :, :128], gw[None, :, 128:256], gw[None, :, 256:]


def solution(mesh):
    row = P(("dp", "expert"), None)
    wide = P("expert", "dp", None)
    return jax.shard_map(
        shards,
        mesh=mesh,
        in_specs=(row, row, row, row, wide, wide, wide),
        out_specs=(row, row, wide, wide, wide),
        check_vma=False,
    )
```

time: 664 us -> 110 us (0.17); the launches traced: 654 us -> 110 us
  waiting for transfers between devices: 568 us -> 0 us
  Pallas kernels: 0 us -> 106 us
  matrix products: 32.3 us -> 0 us
  blocking collectives: 20.5 us -> 0 us
  between operations: 14.4 us -> 0.65 us
  local copies, waits for them, and re-layouts: 11.1 us -> 3.02 us
  other arithmetic: 7.01 us -> 0 us
    all_gather x4 -> x0, waiting for transfers between devices: 284 us -> none  [the longest x1 121 us: shards(): lax.all_gather(w, 'expert', axis=0, tiled=False, axis_index_groups=Y_GROUPS)]
    reduce_scatter x2 -> x0, waiting for transfers between devices: 190 us -> none  [the longest x1 127 us: shards(): lax.psum_scatter(g, 'expert', scatter_dimension=0, tiled=False, axis_inde...]
    pallas_call x0 -> x1, Pallas kernels: none -> 106 us  [call(): pl.pallas_call(kernel, out_shape=out, in_specs=[vm] * 7, out_specs=(vm,)...]
    unnamed x10 -> x0, waiting for transfers between devices: 94.8 us -> none
    dot_general x20 -> x0, matrix products: 32.3 us -> none  [mult(): lax.dot_general(left, right, (dims, ((), ())), preferred_element_type=jnp...]
    all_gather x1 -> x0, blocking collectives: 20.5 us -> none  [shards(): lax.all_gather(gate_mat, 'expert', axis=0, tiled=True, axis_index_groups=...]
    unnamed x20 -> x6, local copies, waits for them, and re-layouts: 9.94 us -> 1.25 us
  transfers between devices with their start and end apart: 8 -> 0, of which waited for: 8 -> 0; matrix products, arithmetic and copies ran while one was open for 4% -> 0% of each run, Pallas kernels for 0% -> 0%
where the time goes in v3:
time: 110 us
  Pallas kernels  106 us (96%)
  local copies, waits for them, and re-layouts  3.02 us (3%)
    pallas_call x1, Pallas kernels, call(): pl.pallas_call(kernel, out_shape=out, in_specs=[vm] * 7, out_specs=(vm,)...  106 us

profile of v3, /device:TPU:1, one launch (start us, length us, event | category | flops | bytes accessed | tf_op | source)
XLA Modules:
  0.0 109.6 jit_solution(13461092500921480036)
XLA Ops:
  0.6 106.0 %shard_map.110 = (bf16[16,3584]{1,0:T(8,128)(2,1)}, f32[2,16]{1,0:T(2,128)}, bf16[448,384]{1,0:T(8,128)(2,1)}) custom-call(bf16[16,3584]{1,0:T(8,128)(2,1)} %tok.1, bf16[16,3584]{1,0:T(8,128)(2,1)} %cot.1, s32[2,16]{1,0:T(2,128)} %bitcast.10, bf16[2,16]{1,0:T(2,128)(2,1)} %bitcast.11, bf16[1,448,128]{2,1,0:T(8,128)(2,1)} %wg.1, bf16[1,448,128]{2,1,0:T(8,128)(2,1)} %wu.1, ...), custom_call_target="tpu_custom_call" | custom-call | flops 7600000000 | bytes 2000000 | tf_op jit(solution)/shard_map/pallas_call | solution.py:529
  106.6 0.0 copy-start
  106.6 1.8 %slice_bitcast_fusion = (bf16[1,448,128]{2,1,0:T(8,128)(2,1)}, bf16[1,448,128]{2,1,0:T(8,128)(2,1)}, bf16[1,448,128]{2,1,0:T(8,128)(2,1)}) fusion(bf16[448,384]{1,0:T(8,128)(2,1)} %get-tuple-element.10), kind=kLoop, calls=%fused_computation | loop fusion | bytes 688128 | tf_op jit(solution)/shard_map/broadcast_in_dim | solution.py:544
  108.4 0.0 copy-done
  108.4 0.0 copy-start.1
  108.4 0.6 copy.14
  109.0 0.0 copy-done.1
  109.1 0.6 copy.15
Async XLA Ops:
  106.6 1.8 %copy-start = (bf16[16,3584]{1,0:T(8,128)(2,1)S(1)}, bf16[16,3584]{1,0:T(8,128)(2,1)}, u32[]{:S(2)}) copy-start(bf16[16,3584]{1,0:T(8,128)(2,1)} %get-tuple-element.19) | copy-start | bytes 344068
  108.4 0.7 copy-start.1

commit v4 on v3

--- a/solution.py
+++ b/solution.py
@@ -23,27 +23,31 @@
 MESH = pl.DeviceIdType.MESH
 BF = jnp.bfloat16
 F32 = jnp.float32
-N_SEM = 320
+N_SEM = 352
 
 ORDER = (
-    ("fy", 0), ("fx", 0), ("el", 2, 1), ("el", 3, 1), ("fx", 2), ("fx", 3), ("ty",), ("tx",), ("fx", 1), ("fy", 2),
-    ("el", 0, 2), ("dw", 0), ("q10", "s"), ("p10", "s"), ("p12", "s"), ("p11", "s"), ("el", 1, 2), ("dw", 1),
-    ("q11", "s"), ("el", 2, 2), ("dw", 2), ("p10", "r", 1), ("q12", "s"), ("p10", "r", 0), ("q10", "r", 0),
-    ("p12", "r", 1), ("q11", "r", 1), ("p12", "r", 0), ("q11", "r", 0), ("q10", "r", 1), ("el", 3, 2), ("dx", 1),
-    ("hs", 1), ("p11", "r", 1), ("dx", 0), ("hs", 0), ("dw", 3), ("h", 1, 1, 1, 1), ("h", 1, 0, 0, 1),
-    ("h", 0, 1, 0, 1), ("h", 0, 1, 1, 1), ("q13", "s"), ("h", 1, 1, 0, 1), ("h", 1, 0, 1, 1), ("p10", "e"),
-    ("p2", "s"), ("h", 0, 0, 0, 1), ("p11", "r", 0), ("h", 1, 1, 1, 2), ("h", 0, 0, 1, 1), ("h", 1, 0, 0, 2),
-    ("q12", "r", 0), ("h", 0, 1, 1, 2), ("h", 0, 1, 0, 2), ("p13", "s"), ("q12", "r", 1), ("h", 1, 0, 1, 2),
-    ("h", 1, 1, 0, 2), ("h", 1, 1, 1, 3), ("p12", "e"), ("h", 0, 0, 0, 2), ("h", 0, 0, 1, 2), ("q11", "e"),
-    ("h", 1, 0, 0, 3), ("h", 0, 1, 1, 3), ("q10", "e"), ("h", 0, 1, 0, 3), ("h", 1, 0, 1, 3), ("h", 1, 1, 0, 3),
-    ("q2", "s"), ("q13", "r", 0), ("q13", "r", 1), ("h", 1, 1, 1, 4), ("h", 0, 0, 1, 3), ("h", 0, 0, 0, 3),
-    ("h", 1, 0, 0, 4), ("p11", "e"), ("h", 0, 1, 1, 4), ("h", 0, 1, 0, 4), ("p2", "r", 1), ("h", 1, 0, 1, 4),
-    ("p2", "r", 0), ("h", 1, 1, 1, 5), ("h", 0, 0, 0, 4), ("h", 1, 1, 0, 4), ("p13", "r", 0), ("h", 0, 0, 1, 4),
-    ("p13", "r", 1), ("h", 1, 0, 0, 5), ("h", 0, 1, 1, 5), ("h", 0, 1, 0, 5), ("h", 1, 0, 1, 5), ("h", 0, 0, 0, 5),
-    ("q2", "r", 0), ("h", 1, 1, 1, 6), ("h", 1, 1, 0, 5), ("q12", "e"), ("q2", "r", 1), ("h", 1, 0, 0, 6),
-    ("h", 0, 0, 1, 5), ("h", 0, 1, 1, 6), ("h", 0, 1, 0, 6), ("h", 1, 0, 1, 6), ("h", 0, 0, 0, 6),
-    ("h", 1, 1, 1, 7), ("h", 1, 1, 0, 6), ("h", 0, 0, 1, 6), ("h", 1, 0, 0, 7), ("p13", "e"), ("h", 0, 1, 1, 7),
-    ("q13", "e"), ("h", 0, 0, 0, 7), ("l1",), ("l0",), ("q2", "e"), ("p2", "e"),
+    ("fy", 0), ("fx", 0), ("tx",), ("fy", 2), ("fx", 2), ("fx", 3), ("fx", 1), ("el", 0, 1), ("el", 1, 1), ("el", 2, 1), ("el", 3, 1), ("ty",),
+    ("el", 0, 2), ("dw", 0), ("p11", "s"), ("p13", "s"), ("q10", "s"), ("q10", "d", 1), ("q10", "d", 0),
+    ("p10", "s"), ("p12", "s"), ("el", 1, 2), ("dw", 1), ("p10", "d", 0), ("p12", "d", 0), ("p13", "d", 0),
+    ("q11", "s"), ("q11", "d", 0), ("el", 2, 2), ("el", 3, 2), ("dx", 0), ("hs", 0), ("dx", 1), ("hs", 1),
+    ("q10", "r", 0), ("q10", "r", 1), ("p13", "r", 0), ("dw", 2), ("h", 0, 1, 0, 1), ("h", 0, 0, 1, 1),
+    ("h", 0, 0, 0, 1), ("h", 0, 1, 1, 1), ("h", 1, 1, 0, 1), ("h", 1, 1, 1, 1), ("q11", "r", 0), ("h", 1, 0, 0, 1),
+    ("h", 1, 0, 1, 1), ("p10", "d", 1), ("p10", "r", 1), ("p11", "d", 1), ("p11", "r", 1), ("q12", "s"),
+    ("p12", "d", 1), ("p12", "r", 1), ("p13", "d", 1), ("p12", "r", 0), ("h", 0, 0, 1, 2), ("p10", "r", 0),
+    ("h", 0, 0, 0, 2), ("h", 0, 1, 1, 2), ("q12", "d", 1), ("p11", "d", 0), ("h", 1, 1, 0, 2), ("h", 1, 1, 1, 2),
+    ("p11", "r", 0), ("h", 1, 0, 0, 2), ("h", 1, 0, 1, 2), ("h", 0, 1, 0, 2), ("q12", "d", 0), ("p13", "r", 1),
+    ("q11", "d", 1), ("q11", "r", 1), ("q10", "e"), ("q2", "s"), ("h", 0, 0, 1, 3), ("h", 0, 0, 0, 3),
+    ("h", 0, 1, 1, 3), ("q12", "r", 0), ("h", 1, 1, 1, 3), ("h", 1, 1, 0, 3), ("q12", "r", 1), ("h", 1, 0, 0, 3),
+    ("h", 1, 0, 1, 3), ("dw", 3), ("h", 0, 1, 0, 3), ("h", 0, 1, 1, 4), ("h", 0, 0, 0, 4), ("h", 1, 1, 0, 4),
+    ("h", 1, 1, 1, 4), ("q13", "s"), ("q13", "d", 0), ("q13", "d", 1), ("h", 1, 0, 0, 4), ("h", 1, 0, 1, 4),
+    ("p10", "e"), ("p2", "s"), ("h", 0, 0, 1, 4), ("q11", "e"), ("q2", "d", 0), ("h", 0, 1, 0, 4),
+    ("h", 0, 1, 1, 5), ("q12", "e"), ("h", 1, 1, 1, 5), ("h", 0, 0, 0, 5), ("q2", "d", 1), ("p12", "e"),
+    ("h", 1, 0, 1, 5), ("h", 1, 0, 0, 5), ("p11", "e"), ("h", 0, 0, 1, 5), ("q13", "r", 1), ("p2", "d", 0),
+    ("h", 1, 1, 0, 5), ("h", 0, 1, 1, 6), ("p2", "d", 1), ("h", 0, 1, 0, 5), ("q2", "r", 0), ("h", 1, 1, 1, 6),
+    ("h", 0, 0, 0, 6), ("q13", "r", 0), ("p13", "e"), ("h", 1, 0, 0, 6), ("h", 1, 0, 1, 6), ("p2", "r", 1),
+    ("h", 0, 0, 1, 6), ("p2", "r", 0), ("h", 1, 1, 0, 6), ("h", 0, 1, 1, 7), ("q2", "r", 1), ("h", 0, 1, 0, 6),
+    ("h", 1, 1, 1, 7), ("h", 0, 0, 0, 7), ("h", 1, 0, 0, 7), ("q13", "e"), ("l1",), ("p2", "e"), ("q2", "e"),
+    ("l0",),
 )
 
 
@@ -55,9 +59,9 @@
     return lax.rem(value + size, size)
 
 
-def kernel(tok, cot, ids, gates, wg, wu, wd, dx_out, part_out, gw,
+def kernel(tok_hbm, cot_hbm, ids, gates, wg_hbm, wu_hbm, wd_hbm, dx_out, part_out, gw,
            xs, ys, stage, w, xt, yt, pre_s, pre_r, back_s, back_r, joined, g, dxs, land,
-           q1rel, q1fin, p1rel, p1fin, rel2, fin2, part_acc, fin, leave, ssem, rsem):
+           q1rel, q1fin, p1rel, p1fin, rel2, fin2, part_acc, fin, leave, tok, cot, wg, wu, wd, insem, ssem, rsem):
     dp = lax.axis_index("dp")
     ex = lax.axis_index("expert")
     x, c = lax.div(dp, NC), lax.rem(dp, NC)
@@ -73,6 +77,14 @@
     z_next = (dev(x, c, y, wrap(z + 1, NZ)), dev(x, c, y, wrap(z - 1, NZ)))
     sibling = dev(x, other, y, z)
 
+    loads = [
+        pltpu.make_async_copy(src, dst, insem.at[i])
+        for i, (src, dst) in enumerate(
+            ((wg_hbm, wg), (wu_hbm, wu), (wd_hbm, wd), (tok_hbm, tok), (cot_hbm, cot)))
+    ]
+    for load in loads:
+        load.start()
+
     barrier = pltpu.get_barrier_semaphore()
     for target in (*x_next, *y_next, *z_next, sibling):
         pl.semaphore_signal(barrier, inc=1, device_id=target, device_id_type=MESH)
@@ -109,6 +121,8 @@
             for h in range(NC)
         ]
 
+    for load in loads:
+        load.wait()
     w[y, x, :, :, 0:128] = wg[0].reshape(4, QR, 128)
     w[y, x, :, :, 128:256] = wu[0].reshape(4, QR, 128)
     w[y, x, :, :, 256:384] = wd[0].reshape(4, QR, 128)
@@ -178,13 +192,11 @@
 
     def z_step(k, between=()):
         jobs = list(between)
-        for p in (0, 1):
-            for n in range(len(PARTS)):
-                z_one(n, p, k)
-                if jobs:
-                    jobs.pop(0)()
-        for job in jobs:
-            job()
+        turns = [(n, p) for p in (0, 1) for n in range(len(PARTS))]
+        for turn, (n, p) in enumerate(turns):
+            z_one(n, p, k)
+            for _ in range(-(-len(jobs) // (len(turns) - turn))):
+                jobs.pop(0)()
 
     first = (x, y)
     second = (y, x)
@@ -369,10 +381,9 @@
     w_slot_far(3)
     z_step(6, [later(fwd_x, i, 0) for i in range(NY)] + [later(fwd_y, 0, 0), later(fwd_y, 2, 0)])
     gate_share(1)
-    z_step(7, [job for i in range(NY) for job in (later(elementwise, i, 0), later(fwd_x, i, 1))])
-    z_step(8, [
-        later(fwd_y, 0, 1), later(fwd_y, 2, 1), later(transpose, xs, xt, 1), later(transpose, ys, yt, 1),
-        later(token_grads, 0, 0), later(token_grads, 1, 0), later(elementwise, 0, 1), later(elementwise, 1, 1)])
+    z_step(7, [job for i in range(NY) for job in (later(elementwise, i, 0), later(fwd_x, i, 1))]
+           + [later(transpose, xs, xt, 1), later(transpose, ys, yt, 1)])
+    z_step(8, [later(fwd_y, 0, 1), later(fwd_y, 2, 1), later(token_grads, 0, 0), later(token_grads, 1, 0)])
     gate_share(2)
 
     def add(dst, *sources):
@@ -386,20 +397,26 @@
             self.at, self.nexts, self.relays, self.finals = at, nexts, relays, finals
             self.r = [alloc(), alloc()]
             self.f = [alloc(), alloc()]
+            self.g = [alloc(), alloc()]
 
         def start(self):
             for d in (0, 1):
                 send(self.at(2, d, 1), self.relays.at[d], self.r[d], self.nexts[d])
+
+        def direct(self, d):
+            shift = 1 if d == 0 else -1
+            send(self.at(shift, 1 - d, 1), self.finals.at[d, pl.ds(1 - d, 1)], self.g[d], self.nexts[d])
 
         def relay(self, d):
             shift = 1 if d == 0 else -1
             recv(self.relays.at[d], self.r[d])
             add(self.at(shift, d, 1), self.relays.at[d])
-            send(self.at(shift, 0, 2), self.finals.at[d], self.f[d], self.nexts[d])
+            send(self.at(shift, d, 1), self.finals.at[d, pl.ds(d, 1)], self.f[d], self.nexts[d])
 
         def end(self):
             for d in (0, 1):
-                recv(self.finals.at[d], self.f[d])
+                recv(self.finals.at[d, pl.ds(1 - d, 1)], self.g[d])
+                recv(self.finals.at[d, pl.ds(d, 1)], self.f[d])
             add(self.at(0, 0, 2), self.finals.at[0], self.finals.at[1])
 
     order_x = tuple(pos(x, shift) for shift in (2, 1, -1, 0))
@@ -477,7 +494,8 @@
     rings.update({"p2": p2, "q2": q2})
     for name, *rest in ORDER:
         if name in rings:
-            {"s": rings[name].start, "r": rings[name].relay, "e": rings[name].end}[rest[0]](*rest[1:])
+            ring = rings[name]
+            {"s": ring.start, "d": ring.direct, "r": ring.relay, "e": ring.end}[rest[0]](*rest[1:])
         else:
             jobs[name](*rest)
 
@@ -494,6 +512,7 @@
 
 def call(tok, cot, ids, gates, wg, wu, wd):
     vm = pl.BlockSpec(memory_space=pltpu.VMEM)
+    hbm = pl.BlockSpec(memory_space=pltpu.HBM)
     out = (
         jax.ShapeDtypeStruct((ROWS, D), BF),
         jax.ShapeDtypeStruct((2, ROWS), F32),
@@ -523,13 +542,16 @@
         pltpu.VMEM((TOK, LANES), F32),
         pltpu.VMEM((NC, ROWS, DH), BF),
         pltpu.VMEM((ROWS, DH), BF),
+        *[pltpu.VMEM((ROWS, D), BF)] * 2,
+        *[pltpu.VMEM((1, 4 * QR, 128), BF)] * 3,
+        pltpu.SemaphoreType.DMA((5,)),
         pltpu.SemaphoreType.DMA((N_SEM,)),
         pltpu.SemaphoreType.DMA((N_SEM,)),
     ]
     return pl.pallas_call(
         kernel,
         out_shape=out,
-        in_specs=[vm] * 7,
+        in_specs=[hbm] * 2 + [vm] * 2 + [hbm] * 3,
         out_specs=(vm,) * 3,
         scratch_shapes=scratch,
         compiler_params=pltpu.CompilerParams(

time: 110 us -> 107 us (0.973)
  Pallas kernels: 106 us -> 104 us
    pallas_call x1, Pallas kernels: 106 us -> 104 us  [call(): pl.pallas_call(kernel, out_shape=out, in_specs=[hbm] * 2 + [vm] * 2 + [hb...]
where the time goes in v4:
time: 107 us
  Pallas kernels  104 us (97%)
  local copies, waits for them, and re-layouts  3.02 us (3%)
    pallas_call x1, Pallas kernels, call(): pl.pallas_call(kernel, out_shape=out, in_specs=[hbm] * 2 + [vm] * 2 + [hb...  104 us

profile of v4, /device:TPU:1, one launch (start us, length us, event | category | flops | bytes accessed | tf_op | source)
XLA Modules:
  0.0 107.3 jit_solution(5267630401710850169)
XLA Ops:
  0.6 103.6 %shard_map.110 = (bf16[16,3584]{1,0:T(8,128)(2,1)}, f32[2,16]{1,0:T(2,128)}, bf16[448,384]{1,0:T(8,128)(2,1)}) custom-call(bf16[16,3584]{1,0:T(8,128)(2,1)} %tok_hbm.1, bf16[16,3584]{1,0:T(8,128)(2,1)} %cot_hbm.1, s32[2,16]{1,0:T(2,128)} %bitcast.10, bf16[2,16]{1,0:T(2,128)(2,1)} %bitcast.11, bf16[1,448,128]{2,1,0:T(8,128)(2,1)} %wg_hbm.1, ...), custom_call_target="tpu_custom_call" | custom-call | flops 7600000000 | bytes 2000000 | tf_op jit(solution)/shard_map/pallas_call | solution.py:551
  104.2 0.0 copy-start
  104.3 1.8 %slice_bitcast_fusion = (bf16[1,448,128]{2,1,0:T(8,128)(2,1)}, bf16[1,448,128]{2,1,0:T(8,128)(2,1)}, bf16[1,448,128]{2,1,0:T(8,128)(2,1)}) fusion(bf16[448,384]{1,0:T(8,128)(2,1)} %get-tuple-element.10), kind=kLoop, calls=%fused_computation | loop fusion | bytes 688128 | tf_op jit(solution)/shard_map/broadcast_in_dim | solution.py:566
  106.0 0.0 copy-done
  106.0 0.0 copy-start.1
  106.0 0.6 copy.14
  106.7 0.0 copy-done.1
  106.7 0.6 copy.15
Async XLA Ops:
  104.2 1.8 %copy-start = (bf16[16,3584]{1,0:T(8,128)(2,1)S(1)}, bf16[16,3584]{1,0:T(8,128)(2,1)}, u32[]{:S(2)}) copy-start(bf16[16,3584]{1,0:T(8,128)(2,1)} %get-tuple-element.19) | copy-start | bytes 344068
  106.0 0.7 copy-start.1

commit v5 on v4

--- a/solution.py
+++ b/solution.py
@@ -26,28 +26,28 @@
 N_SEM = 352
 
 ORDER = (
-    ("fy", 0), ("fx", 0), ("tx",), ("fy", 2), ("fx", 2), ("fx", 3), ("fx", 1), ("el", 0, 1), ("el", 1, 1), ("el", 2, 1), ("el", 3, 1), ("ty",),
-    ("el", 0, 2), ("dw", 0), ("p11", "s"), ("p13", "s"), ("q10", "s"), ("q10", "d", 1), ("q10", "d", 0),
-    ("p10", "s"), ("p12", "s"), ("el", 1, 2), ("dw", 1), ("p10", "d", 0), ("p12", "d", 0), ("p13", "d", 0),
-    ("q11", "s"), ("q11", "d", 0), ("el", 2, 2), ("el", 3, 2), ("dx", 0), ("hs", 0), ("dx", 1), ("hs", 1),
-    ("q10", "r", 0), ("q10", "r", 1), ("p13", "r", 0), ("dw", 2), ("h", 0, 1, 0, 1), ("h", 0, 0, 1, 1),
-    ("h", 0, 0, 0, 1), ("h", 0, 1, 1, 1), ("h", 1, 1, 0, 1), ("h", 1, 1, 1, 1), ("q11", "r", 0), ("h", 1, 0, 0, 1),
-    ("h", 1, 0, 1, 1), ("p10", "d", 1), ("p10", "r", 1), ("p11", "d", 1), ("p11", "r", 1), ("q12", "s"),
-    ("p12", "d", 1), ("p12", "r", 1), ("p13", "d", 1), ("p12", "r", 0), ("h", 0, 0, 1, 2), ("p10", "r", 0),
-    ("h", 0, 0, 0, 2), ("h", 0, 1, 1, 2), ("q12", "d", 1), ("p11", "d", 0), ("h", 1, 1, 0, 2), ("h", 1, 1, 1, 2),
-    ("p11", "r", 0), ("h", 1, 0, 0, 2), ("h", 1, 0, 1, 2), ("h", 0, 1, 0, 2), ("q12", "d", 0), ("p13", "r", 1),
-    ("q11", "d", 1), ("q11", "r", 1), ("q10", "e"), ("q2", "s"), ("h", 0, 0, 1, 3), ("h", 0, 0, 0, 3),
-    ("h", 0, 1, 1, 3), ("q12", "r", 0), ("h", 1, 1, 1, 3), ("h", 1, 1, 0, 3), ("q12", "r", 1), ("h", 1, 0, 0, 3),
-    ("h", 1, 0, 1, 3), ("dw", 3), ("h", 0, 1, 0, 3), ("h", 0, 1, 1, 4), ("h", 0, 0, 0, 4), ("h", 1, 1, 0, 4),
-    ("h", 1, 1, 1, 4), ("q13", "s"), ("q13", "d", 0), ("q13", "d", 1), ("h", 1, 0, 0, 4), ("h", 1, 0, 1, 4),
-    ("p10", "e"), ("p2", "s"), ("h", 0, 0, 1, 4), ("q11", "e"), ("q2", "d", 0), ("h", 0, 1, 0, 4),
-    ("h", 0, 1, 1, 5), ("q12", "e"), ("h", 1, 1, 1, 5), ("h", 0, 0, 0, 5), ("q2", "d", 1), ("p12", "e"),
-    ("h", 1, 0, 1, 5), ("h", 1, 0, 0, 5), ("p11", "e"), ("h", 0, 0, 1, 5), ("q13", "r", 1), ("p2", "d", 0),
-    ("h", 1, 1, 0, 5), ("h", 0, 1, 1, 6), ("p2", "d", 1), ("h", 0, 1, 0, 5), ("q2", "r", 0), ("h", 1, 1, 1, 6),
-    ("h", 0, 0, 0, 6), ("q13", "r", 0), ("p13", "e"), ("h", 1, 0, 0, 6), ("h", 1, 0, 1, 6), ("p2", "r", 1),
-    ("h", 0, 0, 1, 6), ("p2", "r", 0), ("h", 1, 1, 0, 6), ("h", 0, 1, 1, 7), ("q2", "r", 1), ("h", 0, 1, 0, 6),
-    ("h", 1, 1, 1, 7), ("h", 0, 0, 0, 7), ("h", 1, 0, 0, 7), ("q13", "e"), ("l1",), ("p2", "e"), ("q2", "e"),
-    ("l0",),
+    ("fx", 0), ("ty",), ("fy", 0), ("fy", 2), ("fx", 2), ("fx", 3), ("fx", 1), ("el", 0, 1), ("el", 1, 1),
+    ("el", 2, 1), ("el", 3, 1), ("tx",), ("el", 0, 2), ("dw", 0), ("el", 1, 2), ("q10", "s"), ("p12", "s"),
+    ("q10", "d", 1), ("p11", "s"), ("el", 2, 2), ("el", 3, 2), ("dx", 1), ("q10", "d", 0), ("hs", 1), ("dx", 0),
+    ("hs", 0), ("p10", "s"), ("dw", 1), ("q10", "r", 0), ("h", 1, 1, 1, 1), ("p12", "d", 0), ("p12", "r", 0),
+    ("q10", "r", 1), ("h", 1, 0, 1, 1), ("p10", "d", 0), ("p11", "d", 0), ("h", 0, 1, 1, 1), ("p11", "r", 0),
+    ("h", 1, 1, 0, 1), ("h", 0, 0, 1, 1), ("h", 0, 0, 0, 1), ("q11", "s"), ("q11", "d", 1), ("h", 1, 0, 0, 1),
+    ("h", 0, 1, 0, 1), ("p10", "r", 0), ("p13", "s"), ("h", 1, 1, 1, 2), ("q11", "d", 0), ("dw", 2),
+    ("h", 1, 1, 0, 2), ("h", 0, 0, 1, 2), ("h", 0, 0, 0, 2), ("h", 0, 1, 1, 2), ("h", 1, 0, 0, 2),
+    ("h", 1, 0, 1, 2), ("p12", "d", 1), ("p12", "r", 1), ("q11", "r", 0), ("q11", "r", 1), ("q10", "e"),
+    ("q2", "s"), ("q12", "s"), ("h", 0, 1, 0, 2), ("p10", "d", 1), ("p10", "r", 1), ("h", 1, 1, 0, 3),
+    ("h", 0, 0, 1, 3), ("h", 1, 1, 1, 3), ("h", 0, 0, 0, 3), ("h", 0, 1, 1, 3), ("q12", "d", 1), ("h", 1, 0, 0, 3),
+    ("p11", "d", 1), ("p11", "r", 1), ("h", 1, 0, 1, 3), ("q12", "d", 0), ("dw", 3), ("h", 0, 0, 1, 4),
+    ("h", 0, 1, 0, 3), ("h", 1, 1, 1, 4), ("h", 0, 0, 0, 4), ("q13", "s"), ("h", 0, 1, 1, 4), ("q12", "r", 1),
+    ("h", 1, 0, 0, 4), ("q13", "d", 0), ("h", 1, 0, 1, 4), ("h", 1, 1, 0, 4), ("q11", "e"), ("p12", "e"),
+    ("q13", "d", 1), ("q2", "d", 0), ("p13", "d", 0), ("h", 0, 0, 1, 5), ("h", 0, 1, 0, 4), ("q12", "r", 0),
+    ("h", 1, 1, 1, 5), ("h", 0, 0, 0, 5), ("p13", "d", 1), ("p13", "r", 1), ("h", 0, 1, 1, 5), ("h", 1, 0, 0, 5),
+    ("h", 1, 0, 1, 5), ("h", 1, 1, 0, 5), ("p10", "e"), ("p2", "s"), ("p2", "d", 1), ("q13", "r", 1),
+    ("q13", "r", 0), ("h", 0, 0, 1, 6), ("h", 0, 1, 0, 5), ("q2", "r", 0), ("h", 1, 1, 1, 6), ("h", 0, 0, 0, 6),
+    ("p13", "r", 0), ("h", 0, 1, 1, 6), ("h", 1, 0, 0, 6), ("p11", "e"), ("p2", "d", 0), ("h", 1, 0, 1, 6),
+    ("q12", "e"), ("h", 1, 1, 0, 6), ("q2", "d", 1), ("q2", "r", 1), ("h", 0, 1, 0, 6), ("p2", "r", 1),
+    ("h", 1, 1, 1, 7), ("h", 0, 0, 0, 7), ("p2", "r", 0), ("h", 0, 1, 1, 7), ("h", 1, 0, 0, 7), ("p13", "e"),
+    ("q13", "e"), ("l1",), ("l0",), ("p2", "e"), ("q2", "e"),
 )
 
 

time: 107 us -> 106 us (level)
  Pallas kernels: 104 us -> 102 us
    pallas_call x1, Pallas kernels: 104 us -> 102 us  [call(): pl.pallas_call(kernel, out_shape=out, in_specs=[hbm] * 2 + [vm] * 2 + [hb...]
where the time goes in v5:
time: 106 us; the launch traced here: 105 us
  Pallas kernels  102 us (96%)
  local copies, waits for them, and re-layouts  3.02 us (3%)
    pallas_call x1, Pallas kernels, call(): pl.pallas_call(kernel, out_shape=out, in_specs=[hbm] * 2 + [vm] * 2 + [hb...  102 us

profile of v5, /device:TPU:1, one launch (start us, length us, event | category | flops | bytes accessed | tf_op | source)
XLA Modules:
  0.0 105.3 jit_solution(7909620611373392098)
XLA Ops:
  0.6 101.7 %shard_map.110 = (bf16[16,3584]{1,0:T(8,128)(2,1)}, f32[2,16]{1,0:T(2,128)}, bf16[448,384]{1,0:T(8,128)(2,1)}) custom-call(bf16[16,3584]{1,0:T(8,128)(2,1)} %tok_hbm.1, bf16[16,3584]{1,0:T(8,128)(2,1)} %cot_hbm.1, s32[2,16]{1,0:T(2,128)} %bitcast.10, bf16[2,16]{1,0:T(2,128)(2,1)} %bitcast.11, bf16[1,448,128]{2,1,0:T(8,128)(2,1)} %wg_hbm.1, ...), custom_call_target="tpu_custom_call" | custom-call | flops 7600000000 | bytes 2000000 | tf_op jit(solution)/shard_map/pallas_call | solution.py:551
  102.3 0.0 copy-start
  102.3 1.8 %slice_bitcast_fusion = (bf16[1,448,128]{2,1,0:T(8,128)(2,1)}, bf16[1,448,128]{2,1,0:T(8,128)(2,1)}, bf16[1,448,128]{2,1,0:T(8,128)(2,1)}) fusion(bf16[448,384]{1,0:T(8,128)(2,1)} %get-tuple-element.10), kind=kLoop, calls=%fused_computation | loop fusion | bytes 688128 | tf_op jit(solution)/shard_map/broadcast_in_dim | solution.py:566
  104.1 0.0 copy-done
  104.1 0.0 copy-start.1
  104.1 0.6 copy.14
  104.7 0.0 copy-done.1
  104.8 0.6 copy.15
Async XLA Ops:
  102.3 1.8 %copy-start = (bf16[16,3584]{1,0:T(8,128)(2,1)S(1)}, bf16[16,3584]{1,0:T(8,128)(2,1)}, u32[]{:S(2)}) copy-start(bf16[16,3584]{1,0:T(8,128)(2,1)} %get-tuple-element.19) | copy-start | bytes 344068
  104.1 0.7 copy-start.1
